TPU v7x, 256 devices: a whole 4x4x8 slice. The times are simulated.
256 devices in a mesh: seq: 16 (over x_hi, y, core), fsdp: 16 (over z, x_lo).
Axes of the slice: x: 4 (x_hi: 2, x_lo: 2; x = x_hi * 2 + x_lo), y: 4, z: 8, core: 2. Of those that a mesh axis runs over, the one named last changes fastest.
Arguments:
- query_states: bfloat16 [4096, 4096], P('seq', 'fsdp'), may hold values from -24 to 24
- key_states: bfloat16 [4096, 4096], P('seq', 'fsdp'), may hold values from -6 to 6
- value_states: bfloat16 [4096, 4096], P('seq', 'fsdp'), may hold values from -6 to 6
- positions: int32 [4096], P('seq'), may hold values from 0 to 4095, as said below
- out_weight: bfloat16 [4096, 5120], P('fsdp', 'seq'), may hold values from -1 to 1
- cotangent: bfloat16 [4096, 5120], P('seq', 'fsdp'), may hold values from -0.59765625 to 0.59765625
Outputs:
- attn_output: float32 [4096, 5120], P('seq', 'fsdp')
- grad_queries: float32 [4096, 4096], P('seq', 'fsdp')
- grad_keys: float32 [4096, 4096], P('seq', 'fsdp')
- grad_values: float32 [4096, 4096], P('seq', 'fsdp')
- grad_weight: float32 [4096, 5120], P('fsdp', 'seq')
Inputs may be any that keep to these rules, and one draw needn't show every extreme that they name: A permutation of 0 to 4095; each aligned block of 256 rows holds, in increasing order, the positions of one residue class modulo 4096 // 256.
All inputs are finite; a program needn't handle non-finite values.
Results may differ from a plain program's by a relative error of at most 0.02.
Values may be sent and summed in bfloat16 or wider, within the bound.
A program may use at most 128 MiB of HBM per device.

v0:
```python
import jax
import jax.numpy as jnp
from jax import lax
from jax.sharding import PartitionSpec as P

HEAD_DIM = 128


blocked = -1e30


def shifted(block, axis, distance):
    devices = range(lax.axis_size(axis))
    route = [((i - distance) % len(devices), i) for i in devices]
    return lax.ppermute(block, axis, route)


def split_heads(matrix):
    return matrix.reshape(matrix.shape[0], -1, HEAD_DIM)


def masked_scores(query_rows, key_rows, query_pos, key_pos):
    raw = jnp.einsum(
        "qhd,khd->hqk", query_rows, key_rows, preferred_element_type=jnp.float32
    ) * HEAD_DIM ** (-0.5)
    visible = key_pos[None, None, :] <= query_pos[None, :, None]
    return jnp.where(visible, raw, blocked)


def tile_grads(
    query_rows, grad_rows, log_total, row_delta, query_pos, key_rows, value_rows, key_pos
):
    scores = masked_scores(query_rows, key_rows, query_pos, key_pos)
    probs = jnp.exp(scores - log_total[:, :, None])
    grad_probs = jnp.einsum(
        "qhd,khd->hqk", grad_rows, value_rows, preferred_element_type=jnp.float32
    )
    grad_scores = (probs * (grad_probs - row_delta[:, :, None])).astype(jnp.bfloat16)
    grad_query = jnp.einsum(
        "hqk,khd->qhd", grad_scores, key_rows, preferred_element_type=jnp.float32
    )
    grad_key = jnp.einsum(
        "hqk,qhd->khd", grad_scores, query_rows, preferred_element_type=jnp.float32
    )
    grad_value = jnp.einsum(
        "hqk,qhd->khd", probs.astype(jnp.bfloat16), grad_rows, preferred_element_type=jnp.float32
    )
    return (grad_query, grad_key, grad_value)


def shards(query_states, key_states, value_states, positions, out_weight, cotangent):
    local_tokens = query_states.shape[0]
    query_heads = split_heads(query_states)
    key_heads = split_heads(key_states)
    value_heads = split_heads(value_states)
    local_heads = query_heads.shape[1]
    row_max = jnp.full((local_heads, local_tokens), blocked, jnp.float32)
    piece_keys = lax.all_gather(key_states, "seq", axis=0, tiled=True)
    piece_pos = lax.all_gather(positions, "seq", axis=0, tiled=True)
    scores = masked_scores(query_heads, split_heads(piece_keys), positions, piece_pos)
    new_max = jnp.maximum(row_max, jnp.max(scores, axis=2))
    new_total = jnp.sum(jnp.exp(scores - new_max[:, :, None]), axis=2)
    log_total = new_max + jnp.log(new_total)
    zero_heads = jnp.zeros((local_tokens, local_heads, HEAD_DIM), jnp.float32)
    piece_keys = lax.all_gather(key_states, "seq", axis=0, tiled=True)
    piece_values = lax.all_gather(value_states, "seq", axis=0, tiled=True)
    piece_pos = lax.all_gather(positions, "seq", axis=0, tiled=True)
    scores = masked_scores(query_heads, split_heads(piece_keys), positions, piece_pos)
    weights = jnp.exp(scores - log_total[:, :, None]).astype(jnp.bfloat16)
    attended = jnp.einsum(
        "hqk,khd->qhd", weights, split_heads(piece_values), preferred_element_type=jnp.float32
    )
    attended_heads = attended.astype(jnp.bfloat16)
    attended_flat = attended_heads.reshape(local_tokens, local_heads * HEAD_DIM)
    weight_full = lax.all_gather(out_weight, "seq", axis=1, tiled=True)
    partial_sum = jnp.dot(attended_flat, weight_full, preferred_element_type=jnp.float32).astype(
        jnp.bfloat16
    )
    attn_output = lax.psum_scatter(partial_sum, "fsdp", scatter_dimension=1, tiled=True).astype(
        jnp.float32
    )
    cotangent_full = lax.all_gather(cotangent, "fsdp", axis=1, tiled=True)
    grad_attended = jnp.einsum(
        "td,hd->th", cotangent_full, weight_full, preferred_element_type=jnp.float32
    ).astype(jnp.bfloat16)
    weight_term = jnp.einsum(
        "th,td->hd", attended_flat, cotangent_full, preferred_element_type=jnp.float32
    )
    grad_weight = lax.psum_scatter(weight_term, "seq", scatter_dimension=1, tiled=True)
    grad_heads = split_heads(grad_attended)
    row_delta = jnp.sum(
        grad_heads.astype(jnp.float32) * attended_heads.astype(jnp.float32), axis=2
    ).T
    cycle_length = lax.axis_size("seq")

    def key_step(cycle_step, state_tuple):
        key_block, value_block, key_pos, key_grad, value_grad, query_grad = state_tuple
        grad_query, grad_key, grad_value = tile_grads(
            query_heads,
            grad_heads,
            log_total,
            row_delta,
            positions,
            key_block,
            value_block,
            key_pos,
        )
        key_block, value_block, key_pos = shifted((key_block, value_block, key_pos), "seq", 1)
        key_grad, value_grad = shifted((key_grad + grad_key, value_grad + grad_value), "seq", 1)
        return (key_block, value_block, key_pos, key_grad, value_grad, query_grad + grad_query)

    final_state = lax.fori_loop(
        0,
        cycle_length,
        key_step,
        (key_heads, value_heads, positions, zero_heads, zero_heads, zero_heads),
    )
    query_sum, key_sum, value_sum = (final_state[5], final_state[3], final_state[4])
    score_scale = HEAD_DIM ** (-0.5)
    grad_queries = (query_sum * score_scale).reshape(local_tokens, local_heads * HEAD_DIM)
    grad_keys = (key_sum * score_scale).reshape(local_tokens, local_heads * HEAD_DIM)
    grad_values = value_sum.reshape(local_tokens, local_heads * HEAD_DIM)
    return (attn_output, grad_queries, grad_keys, grad_values, grad_weight)


def solution(mesh):
    in_specs = (
        P("seq", "fsdp"),
        P("seq", "fsdp"),
        P("seq", "fsdp"),
        P("seq"),
        P("fsdp", "seq"),
        P("seq", "fsdp"),
    )
    out_specs = (
        P("seq", "fsdp"),
        P("seq", "fsdp"),
        P("seq", "fsdp"),
        P("seq", "fsdp"),
        P("fsdp", "seq"),
    )
    return jax.shard_map(shards, mesh=mesh, in_specs=in_specs, out_specs=out_specs, check_vma=False)
```

profile of v0, /device:TPU:4, one launch (start us, length us, event | category | flops | bytes accessed | tf_op | source)
XLA Modules:
  0.0 591.6 jit_solution(8603280490069514510)
XLA Ops:
  7.2 0.7 all-gather.8.cloned.1.call-update
  7.9 1.7 copy.37
  9.7 0.7 all-gather.10.cloned.1.call-update
  10.4 0.5 all-gather.12.cloned.1.call-update
  11.0 1.0 copy.36
  12.0 22.1 %all-gather = s32[16,1,256]{2,1,0:T(1,128)S(1)} all-gather(s32[1,1,256]{2,1,0:T(1,128)} %bitcast.94), channel_id=1, replica_groups=mesh['seq'=16,'fsdp'=16] {'seq'}, dimensions={0}, use_global_device_ids=true | all-gather | bytes 17408 | tf_op jit(solution)/shard_map/all_gather | solution.py:67
  34.1 2.3 broadcast_compare_fusion.1
  36.4 27.4 %all-gather.8.cloned.1.call-done = bf16[4096,256]{1,0:T(8,128)(2,1)} async-done(((bf16[256,256]{1,0:T(8,128)(2,1)}), bf16[4096,256]{1,0:T(8,128)(2,1)}) %all-gather.8.cloned.1.call-update) | async-done | bytes 2097168 | tf_op jit(solution)/shard_map/all_gather | solution.py:66
  63.9 2.9 copy.40
  66.8 51.1 %all-gather.6.cloned.1.call-done = bf16[4096,256]{0,1:T(8,128)(2,1)} async-done(((bf16[256,256]{0,1:T(8,128)(2,1)}), bf16[4096,256]{0,1:T(8,128)(2,1)}) %all-gather.6.cloned.1.call-update) | async-done | bytes 2097168 | tf_op jit(solution)/shard_map/all_gather | solution.py:65
  117.9 4.1 fusion.12
  122.0 1.3 exponential_reduce_fusion
  123.3 2.0 copy-done
  125.3 47.9 %all-gather.10.cloned.1.call-done = bf16[256,5120]{0,1:T(8,128)(2,1)} async-done(((bf16[256,320]{0,1:T(8,128)(2,1)}), bf16[256,5120]{0,1:T(8,128)(2,1)}) %all-gather.10.cloned.1.call-update) | async-done | bytes 2621456 | tf_op jit(solution)/shard_map/all_gather | solution.py:75
  173.2 79.6 %all-gather.12.cloned.1.call-done = bf16[256,5120]{0,1:T(8,128)(2,1)} async-done(((bf16[256,320]{0,1:T(8,128)(2,1)}), bf16[256,5120]{0,1:T(8,128)(2,1)}) %all-gather.12.cloned.1.call-update) | async-done | bytes 2621456 | tf_op jit(solution)/shard_map/all_gather | solution.py:82
  252.8 3.7 convolution_convert_fusion.1
  256.4 5.2 multiply_reduce_fusion
  261.6 2.3 convolution_convert_fusion
  264.3 0.5 copy-done.5
  265.2 1.0 copy.46
  266.3 3.2 fusion.13
  269.5 311.3 %while.21 = (s32[]{:T(128)}, bf16[256,2,128]{2,0,1:T(8,128)(2,1)S(1)}, bf16[256,2,128]{2,0,1:T(8,128)(2,1)S(1)}, s32[256]{0:T(256)S(1)}, f32[256,2,128]{2,0,1:T(...) while((s32[]{:T(128)}, ...), condition=%wide.region_5.6_spmd.clone, body=%wide.region_4.5_spmd.clone.sunk | while | flops 169017344 | bytes 8663383 | solution.py:112
  270.6 0.3 fusion.61
  270.9 0.7 collective-permute-start.4
  271.7 2.5 collective-permute-start.1
  274.5 39.1 %collective-permute-done.2 = s32[256]{0:T(256)S(1)} collective-permute-done((s32[256]{0:T(256)S(1)}, s32[256]{0:T(256)S(1)}, u32[]{:S(2)}, u32[]{:S(2)}) %collective-permute-start.2) | collective-permute-done | bytes 1056 | tf_op jit(solution)/shard_map/while/body/eval_jaxpr/ppermute | solution.py:15
  314.7 0.3 fusion.61
  315.7 31.4 %collective-permute-done.2 = s32[256]{0:T(256)S(1)} collective-permute-done((s32[256]{0:T(256)S(1)}, s32[256]{0:T(256)S(1)}, u32[]{:S(2)}, u32[]{:S(2)}) %collective-permute-start.2) | collective-permute-done | bytes 1056 | tf_op jit(solution)/shard_map/while/body/eval_jaxpr/ppermute | solution.py:15
  347.8 0.3 fusion.60
  348.2 0.3 fusion.61
  349.1 14.1 %collective-permute-done.2 = s32[256]{0:T(256)S(1)} collective-permute-done((s32[256]{0:T(256)S(1)}, s32[256]{0:T(256)S(1)}, u32[]{:S(2)}, u32[]{:S(2)}) %collective-permute-start.2) | collective-permute-done | bytes 1056 | tf_op jit(solution)/shard_map/while/body/eval_jaxpr/ppermute | solution.py:15
  364.3 0.3 fusion.61
  365.3 14.1 %collective-permute-done.2 = s32[256]{0:T(256)S(1)} collective-permute-done((s32[256]{0:T(256)S(1)}, s32[256]{0:T(256)S(1)}, u32[]{:S(2)}, u32[]{:S(2)}) %collective-permute-start.2) | collective-permute-done | bytes 1056 | tf_op jit(solution)/shard_map/while/body/eval_jaxpr/ppermute | solution.py:15
  380.1 0.3 fusion.60
  380.5 0.3 fusion.61
  381.4 21.3 %collective-permute-done.2 = s32[256]{0:T(256)S(1)} collective-permute-done((s32[256]{0:T(256)S(1)}, s32[256]{0:T(256)S(1)}, u32[]{:S(2)}, u32[]{:S(2)}) %collective-permute-start.2) | collective-permute-done | bytes 1056 | tf_op jit(solution)/shard_map/while/body/eval_jaxpr/ppermute | solution.py:15
  403.7 0.3 fusion.61
  404.7 14.2 %collective-permute-done.2 = s32[256]{0:T(256)S(1)} collective-permute-done((s32[256]{0:T(256)S(1)}, s32[256]{0:T(256)S(1)}, u32[]{:S(2)}, u32[]{:S(2)}) %collective-permute-start.2) | collective-permute-done | bytes 1056 | tf_op jit(solution)/shard_map/while/body/eval_jaxpr/ppermute | solution.py:15
  420.0 0.3 fusion.61
  420.9 14.5 %collective-permute-done.2 = s32[256]{0:T(256)S(1)} collective-permute-done((s32[256]{0:T(256)S(1)}, s32[256]{0:T(256)S(1)}, u32[]{:S(2)}, u32[]{:S(2)}) %collective-permute-start.2) | collective-permute-done | bytes 1056 | tf_op jit(solution)/shard_map/while/body/eval_jaxpr/ppermute | solution.py:15
  436.2 0.3 fusion.60
  436.5 0.3 fusion.61
  437.4 14.2 %collective-permute-done.2 = s32[256]{0:T(256)S(1)} collective-permute-done((s32[256]{0:T(256)S(1)}, s32[256]{0:T(256)S(1)}, u32[]{:S(2)}, u32[]{:S(2)}) %collective-permute-start.2) | collective-permute-done | bytes 1056 | tf_op jit(solution)/shard_map/while/body/eval_jaxpr/ppermute | solution.py:15
  452.4 0.3 fusion.60
  452.8 0.3 fusion.61
  453.7 14.1 %collective-permute-done.2 = s32[256]{0:T(256)S(1)} collective-permute-done((s32[256]{0:T(256)S(1)}, s32[256]{0:T(256)S(1)}, u32[]{:S(2)}, u32[]{:S(2)}) %collective-permute-start.2) | collective-permute-done | bytes 1056 | tf_op jit(solution)/shard_map/while/body/eval_jaxpr/ppermute | solution.py:15
  468.9 0.3 fusion.61
  469.9 14.1 %collective-permute-done.2 = s32[256]{0:T(256)S(1)} collective-permute-done((s32[256]{0:T(256)S(1)}, s32[256]{0:T(256)S(1)}, u32[]{:S(2)}, u32[]{:S(2)}) %collective-permute-start.2) | collective-permute-done | bytes 1056 | tf_op jit(solution)/shard_map/while/body/eval_jaxpr/ppermute | solution.py:15
  485.1 0.3 fusion.61
  486.0 14.1 %collective-permute-done.2 = s32[256]{0:T(256)S(1)} collective-permute-done((s32[256]{0:T(256)S(1)}, s32[256]{0:T(256)S(1)}, u32[]{:S(2)}, u32[]{:S(2)}) %collective-permute-start.2) | collective-permute-done | bytes 1056 | tf_op jit(solution)/shard_map/while/body/eval_jaxpr/ppermute | solution.py:15
  501.2 0.3 fusion.61
  502.1 14.1 %collective-permute-done.2 = s32[256]{0:T(256)S(1)} collective-permute-done((s32[256]{0:T(256)S(1)}, s32[256]{0:T(256)S(1)}, u32[]{:S(2)}, u32[]{:S(2)}) %collective-permute-start.2) | collective-permute-done | bytes 1056 | tf_op jit(solution)/shard_map/while/body/eval_jaxpr/ppermute | solution.py:15
  517.4 0.3 fusion.61
  518.3 14.1 %collective-permute-done.2 = s32[256]{0:T(256)S(1)} collective-permute-done((s32[256]{0:T(256)S(1)}, s32[256]{0:T(256)S(1)}, u32[]{:S(2)}, u32[]{:S(2)}) %collective-permute-start.2) | collective-permute-done | bytes 1056 | tf_op jit(solution)/shard_map/while/body/eval_jaxpr/ppermute | solution.py:15
  533.5 0.3 fusion.61
  534.4 14.1 %collective-permute-done.2 = s32[256]{0:T(256)S(1)} collective-permute-done((s32[256]{0:T(256)S(1)}, s32[256]{0:T(256)S(1)}, u32[]{:S(2)}, u32[]{:S(2)}) %collective-permute-start.2) | collective-permute-done | bytes 1056 | tf_op jit(solution)/shard_map/while/body/eval_jaxpr/ppermute | solution.py:15
  549.7 0.3 fusion.61
  550.6 14.1 %collective-permute-done.2 = s32[256]{0:T(256)S(1)} collective-permute-done((s32[256]{0:T(256)S(1)}, s32[256]{0:T(256)S(1)}, u32[]{:S(2)}, u32[]{:S(2)}) %collective-permute-start.2) | collective-permute-done | bytes 1056 | tf_op jit(solution)/shard_map/while/body/eval_jaxpr/ppermute | solution.py:15
  565.8 0.3 fusion.61
  566.7 14.1 %collective-permute-done.2 = s32[256]{0:T(256)S(1)} collective-permute-done((s32[256]{0:T(256)S(1)}, s32[256]{0:T(256)S(1)}, u32[]{:S(2)}, u32[]{:S(2)}) %collective-permute-start.2) | collective-permute-done | bytes 1056 | tf_op jit(solution)/shard_map/while/body/eval_jaxpr/ppermute | solution.py:15
  581.0 0.7 copy.60
  581.7 0.7 copy.61
  582.4 0.7 copy_bitcast_fusion
  583.1 1.7 convert_element_type.34
  (300 shorter events, 25.4 us)
Async XLA Ops:
  7.2 56.7 %all-gather.8.cloned.1.call-start = ((), (), s32[]{:S(2)}) async-start(), calls=%async_computation.3 | async-start | bytes 2228224 | tf_op jit(solution)/shard_map/all_gather | solution.py:66
  7.9 110.0 %all-gather.6.cloned.1.call-start = ((), (), s32[]{:S(2)}) async-start(), calls=%async_computation.2 | async-start | bytes 2228224 | tf_op jit(solution)/shard_map/all_gather | solution.py:65
  9.6 163.5 %all-gather.10.cloned.1.call-start = ((), (), s32[]{:S(2)}) async-start(), calls=%async_computation.4 | async-start | bytes 2785280 | tf_op jit(solution)/shard_map/all_gather | solution.py:75
  10.4 242.4 %all-gather.12.cloned.1.call-start = ((), (), s32[]{:S(2)}) async-start(), calls=%async_computation.6 | async-start | bytes 2785280 | tf_op jit(solution)/shard_map/all_gather | solution.py:82
  10.9 572.2 %reduce-scatter.3.cloned.1.call-start = ((), (), s32[]{:S(2)}) async-start(), calls=%async_computation.5 | async-start | bytes 2785280 | tf_op jit(solution)/shard_map/reduce_scatter | solution.py:79
  264.0 320.8 %reduce-scatter.5.cloned.1.call-start = ((), (), s32[]{:S(2)}) async-start(), calls=%async_computation.7 | async-start | bytes 5570560 | tf_op jit(solution)/shard_map/reduce_scatter | solution.py:89
  270.5 43.1 %collective-permute-start.3 = (f32[256,2,128]{2,0,1:T(8,128)S(1)}, f32[256,2,128]{2,0,1:T(8,128)S(1)}, u32[]{:S(2)}, u32[]{:S(2)}) collective-permute-start(f32[256,2,128]{2,0,1:T(8,128)S(1)} %fusion.60), channel_id=1, source_target_pairs={{240,0},{0,16},{16,32},{32,48},{48,64},{64,80},{80,96},{96,112},{1... | collective-permute-start | bytes 786440 | tf_op jit(solution)/shard_map/while/body/eval_jaxpr/ppermute | solution.py:15
  270.9 42.8 %collective-permute-start.4 = (f32[256,2,128]{2,0,1:T(8,128)S(1)}, f32[256,2,128]{2,0,1:T(8,128)S(1)}, u32[]{:S(2)}, u32[]{:S(2)}) collective-permute-start(f32[256,2,128]{2,0,1:T(8,128)S(1)} %fusion.61), channel_id=1, source_target_pairs={{240,0},{0,16},{16,32},{32,48},{48,64},{64,80},{80,96},{96,112},{1... | collective-permute-start | bytes 786440 | tf_op jit(solution)/shard_map/while/body/eval_jaxpr/ppermute | solution.py:15
  271.6 42.1 %collective-permute-start = (bf16[256,2,128]{2,0,1:T(8,128)(2,1)S(1)}, bf16[256,2,128]{2,0,1:T(8,128)(2,1)S(1)}, u32[]{:S(2)}, u32[]{:S(2)}) collective-permute-start(bf16[256,2,128]{2,0,1:T(8,128)(2,1)S(1)} %copy.70), channel_id=1, source_target_pairs={{240,0},{0,16},{16,32},{32,48},{48,64},{64,80},{80,96},{96,112},{1... | collective-permute-start | bytes 393224 | tf_op jit(solution)/shard_map/while/body/eval_jaxpr/ppermute | solution.py:15
  271.7 42.0 %collective-permute-start.1 = (bf16[256,2,128]{2,0,1:T(8,128)(2,1)S(1)}, bf16[256,2,128]{2,0,1:T(8,128)(2,1)S(1)}, u32[]{:S(2)}, u32[]{:S(2)}) collective-permute-start(bf16[256,2,128]{2,0,1:T(8,128)(2,1)S(1)} %copy.71), channel_id=1, source_target_pairs={{240,0},{0,16},{16,32},{32,48},{48,64},{64,80},{80,96},{96,112},{1... | collective-permute-start | bytes 393224 | tf_op jit(solution)/shard_map/while/body/eval_jaxpr/ppermute | solution.py:15
  274.2 39.5 %collective-permute-start.2 = (s32[256]{0:T(256)S(1)}, s32[256]{0:T(256)S(1)}, u32[]{:S(2)}, u32[]{:S(2)}) collective-permute-start(s32[256]{0:T(256)S(1)} %copy.72), channel_id=1, source_target_pairs={{240,0},{0,16},{16,32},{32,48},{48,64},{64,80},{80,96},{96,112},{1... | collective-permute-start | bytes 3080 | tf_op jit(solution)/shard_map/while/body/eval_jaxpr/ppermute | solution.py:15
  314.6 32.5 %collective-permute-start.3 = (f32[256,2,128]{2,0,1:T(8,128)S(1)}, f32[256,2,128]{2,0,1:T(8,128)S(1)}, u32[]{:S(2)}, u32[]{:S(2)}) collective-permute-start(f32[256,2,128]{2,0,1:T(8,128)S(1)} %fusion.60), channel_id=1, source_target_pairs={{240,0},{0,16},{16,32},{32,48},{48,64},{64,80},{80,96},{96,112},{1... | collective-permute-start | bytes 786440 | tf_op jit(solution)/shard_map/while/body/eval_jaxpr/ppermute | solution.py:15
  315.0 32.1 %collective-permute-start.4 = (f32[256,2,128]{2,0,1:T(8,128)S(1)}, f32[256,2,128]{2,0,1:T(8,128)S(1)}, u32[]{:S(2)}, u32[]{:S(2)}) collective-permute-start(f32[256,2,128]{2,0,1:T(8,128)S(1)} %fusion.61), channel_id=1, source_target_pairs={{240,0},{0,16},{16,32},{32,48},{48,64},{64,80},{80,96},{96,112},{1... | collective-permute-start | bytes 786440 | tf_op jit(solution)/shard_map/while/body/eval_jaxpr/ppermute | solution.py:15
  315.1 32.0 %collective-permute-start = (bf16[256,2,128]{2,0,1:T(8,128)(2,1)S(1)}, bf16[256,2,128]{2,0,1:T(8,128)(2,1)S(1)}, u32[]{:S(2)}, u32[]{:S(2)}) collective-permute-start(bf16[256,2,128]{2,0,1:T(8,128)(2,1)S(1)} %copy.70), channel_id=1, source_target_pairs={{240,0},{0,16},{16,32},{32,48},{48,64},{64,80},{80,96},{96,112},{1... | collective-permute-start | bytes 393224 | tf_op jit(solution)/shard_map/while/body/eval_jaxpr/ppermute | solution.py:15
  315.2 31.9 %collective-permute-start.1 = (bf16[256,2,128]{2,0,1:T(8,128)(2,1)S(1)}, bf16[256,2,128]{2,0,1:T(8,128)(2,1)S(1)}, u32[]{:S(2)}, u32[]{:S(2)}) collective-permute-start(bf16[256,2,128]{2,0,1:T(8,128)(2,1)S(1)} %copy.71), channel_id=1, source_target_pairs={{240,0},{0,16},{16,32},{32,48},{48,64},{64,80},{80,96},{96,112},{1... | collective-permute-start | bytes 393224 | tf_op jit(solution)/shard_map/while/body/eval_jaxpr/ppermute | solution.py:15
  315.3 31.8 %collective-permute-start.2 = (s32[256]{0:T(256)S(1)}, s32[256]{0:T(256)S(1)}, u32[]{:S(2)}, u32[]{:S(2)}) collective-permute-start(s32[256]{0:T(256)S(1)} %copy.72), channel_id=1, source_target_pairs={{240,0},{0,16},{16,32},{32,48},{48,64},{64,80},{80,96},{96,112},{1... | collective-permute-start | bytes 3080 | tf_op jit(solution)/shard_map/while/body/eval_jaxpr/ppermute | solution.py:15
  348.1 15.2 %collective-permute-start.3 = (f32[256,2,128]{2,0,1:T(8,128)S(1)}, f32[256,2,128]{2,0,1:T(8,128)S(1)}, u32[]{:S(2)}, u32[]{:S(2)}) collective-permute-start(f32[256,2,128]{2,0,1:T(8,128)S(1)} %fusion.60), channel_id=1, source_target_pairs={{240,0},{0,16},{16,32},{32,48},{48,64},{64,80},{80,96},{96,112},{1... | collective-permute-start | bytes 786440 | tf_op jit(solution)/shard_map/while/body/eval_jaxpr/ppermute | solution.py:15
  348.5 14.8 %collective-permute-start.4 = (f32[256,2,128]{2,0,1:T(8,128)S(1)}, f32[256,2,128]{2,0,1:T(8,128)S(1)}, u32[]{:S(2)}, u32[]{:S(2)}) collective-permute-start(f32[256,2,128]{2,0,1:T(8,128)S(1)} %fusion.61), channel_id=1, source_target_pairs={{240,0},{0,16},{16,32},{32,48},{48,64},{64,80},{80,96},{96,112},{1... | collective-permute-start | bytes 786440 | tf_op jit(solution)/shard_map/while/body/eval_jaxpr/ppermute | solution.py:15
  348.5 14.7 %collective-permute-start = (bf16[256,2,128]{2,0,1:T(8,128)(2,1)S(1)}, bf16[256,2,128]{2,0,1:T(8,128)(2,1)S(1)}, u32[]{:S(2)}, u32[]{:S(2)}) collective-permute-start(bf16[256,2,128]{2,0,1:T(8,128)(2,1)S(1)} %copy.70), channel_id=1, source_target_pairs={{240,0},{0,16},{16,32},{32,48},{48,64},{64,80},{80,96},{96,112},{1... | collective-permute-start | bytes 393224 | tf_op jit(solution)/shard_map/while/body/eval_jaxpr/ppermute | solution.py:15
  364.2 15.2 %collective-permute-start.3 = (f32[256,2,128]{2,0,1:T(8,128)S(1)}, f32[256,2,128]{2,0,1:T(8,128)S(1)}, u32[]{:S(2)}, u32[]{:S(2)}) collective-permute-start(f32[256,2,128]{2,0,1:T(8,128)S(1)} %fusion.60), channel_id=1, source_target_pairs={{240,0},{0,16},{16,32},{32,48},{48,64},{64,80},{80,96},{96,112},{1... | collective-permute-start | bytes 786440 | tf_op jit(solution)/shard_map/while/body/eval_jaxpr/ppermute | solution.py:15
  364.6 14.8 %collective-permute-start.4 = (f32[256,2,128]{2,0,1:T(8,128)S(1)}, f32[256,2,128]{2,0,1:T(8,128)S(1)}, u32[]{:S(2)}, u32[]{:S(2)}) collective-permute-start(f32[256,2,128]{2,0,1:T(8,128)S(1)} %fusion.61), channel_id=1, source_target_pairs={{240,0},{0,16},{16,32},{32,48},{48,64},{64,80},{80,96},{96,112},{1... | collective-permute-start | bytes 786440 | tf_op jit(solution)/shard_map/while/body/eval_jaxpr/ppermute | solution.py:15
  364.7 14.7 %collective-permute-start = (bf16[256,2,128]{2,0,1:T(8,128)(2,1)S(1)}, bf16[256,2,128]{2,0,1:T(8,128)(2,1)S(1)}, u32[]{:S(2)}, u32[]{:S(2)}) collective-permute-start(bf16[256,2,128]{2,0,1:T(8,128)(2,1)S(1)} %copy.70), channel_id=1, source_target_pairs={{240,0},{0,16},{16,32},{32,48},{48,64},{64,80},{80,96},{96,112},{1... | collective-permute-start | bytes 393224 | tf_op jit(solution)/shard_map/while/body/eval_jaxpr/ppermute | solution.py:15
  380.4 22.3 %collective-permute-start.3 = (f32[256,2,128]{2,0,1:T(8,128)S(1)}, f32[256,2,128]{2,0,1:T(8,128)S(1)}, u32[]{:S(2)}, u32[]{:S(2)}) collective-permute-start(f32[256,2,128]{2,0,1:T(8,128)S(1)} %fusion.60), channel_id=1, source_target_pairs={{240,0},{0,16},{16,32},{32,48},{48,64},{64,80},{80,96},{96,112},{1... | collective-permute-start | bytes 786440 | tf_op jit(solution)/shard_map/while/body/eval_jaxpr/ppermute | solution.py:15
  380.8 21.9 %collective-permute-start.4 = (f32[256,2,128]{2,0,1:T(8,128)S(1)}, f32[256,2,128]{2,0,1:T(8,128)S(1)}, u32[]{:S(2)}, u32[]{:S(2)}) collective-permute-start(f32[256,2,128]{2,0,1:T(8,128)S(1)} %fusion.61), channel_id=1, source_target_pairs={{240,0},{0,16},{16,32},{32,48},{48,64},{64,80},{80,96},{96,112},{1... | collective-permute-start | bytes 786440 | tf_op jit(solution)/shard_map/while/body/eval_jaxpr/ppermute | solution.py:15
  380.8 21.8 %collective-permute-start = (bf16[256,2,128]{2,0,1:T(8,128)(2,1)S(1)}, bf16[256,2,128]{2,0,1:T(8,128)(2,1)S(1)}, u32[]{:S(2)}, u32[]{:S(2)}) collective-permute-start(bf16[256,2,128]{2,0,1:T(8,128)(2,1)S(1)} %copy.70), channel_id=1, source_target_pairs={{240,0},{0,16},{16,32},{32,48},{48,64},{64,80},{80,96},{96,112},{1... | collective-permute-start | bytes 393224 | tf_op jit(solution)/shard_map/while/body/eval_jaxpr/ppermute | solution.py:15
  380.9 21.7 %collective-permute-start.1 = (bf16[256,2,128]{2,0,1:T(8,128)(2,1)S(1)}, bf16[256,2,128]{2,0,1:T(8,128)(2,1)S(1)}, u32[]{:S(2)}, u32[]{:S(2)}) collective-permute-start(bf16[256,2,128]{2,0,1:T(8,128)(2,1)S(1)} %copy.71), channel_id=1, source_target_pairs={{240,0},{0,16},{16,32},{32,48},{48,64},{64,80},{80,96},{96,112},{1... | collective-permute-start | bytes 393224 | tf_op jit(solution)/shard_map/while/body/eval_jaxpr/ppermute | solution.py:15
  381.0 21.6 %collective-permute-start.2 = (s32[256]{0:T(256)S(1)}, s32[256]{0:T(256)S(1)}, u32[]{:S(2)}, u32[]{:S(2)}) collective-permute-start(s32[256]{0:T(256)S(1)} %copy.72), channel_id=1, source_target_pairs={{240,0},{0,16},{16,32},{32,48},{48,64},{64,80},{80,96},{96,112},{1... | collective-permute-start | bytes 3080 | tf_op jit(solution)/shard_map/while/body/eval_jaxpr/ppermute | solution.py:15
  403.7 15.3 %collective-permute-start.3 = (f32[256,2,128]{2,0,1:T(8,128)S(1)}, f32[256,2,128]{2,0,1:T(8,128)S(1)}, u32[]{:S(2)}, u32[]{:S(2)}) collective-permute-start(f32[256,2,128]{2,0,1:T(8,128)S(1)} %fusion.60), channel_id=1, source_target_pairs={{240,0},{0,16},{16,32},{32,48},{48,64},{64,80},{80,96},{96,112},{1... | collective-permute-start | bytes 786440 | tf_op jit(solution)/shard_map/while/body/eval_jaxpr/ppermute | solution.py:15
  404.0 14.9 %collective-permute-start.4 = (f32[256,2,128]{2,0,1:T(8,128)S(1)}, f32[256,2,128]{2,0,1:T(8,128)S(1)}, u32[]{:S(2)}, u32[]{:S(2)}) collective-permute-start(f32[256,2,128]{2,0,1:T(8,128)S(1)} %fusion.61), channel_id=1, source_target_pairs={{240,0},{0,16},{16,32},{32,48},{48,64},{64,80},{80,96},{96,112},{1... | collective-permute-start | bytes 786440 | tf_op jit(solution)/shard_map/while/body/eval_jaxpr/ppermute | solution.py:15
  404.1 14.8 %collective-permute-start = (bf16[256,2,128]{2,0,1:T(8,128)(2,1)S(1)}, bf16[256,2,128]{2,0,1:T(8,128)(2,1)S(1)}, u32[]{:S(2)}, u32[]{:S(2)}) collective-permute-start(bf16[256,2,128]{2,0,1:T(8,128)(2,1)S(1)} %copy.70), channel_id=1, source_target_pairs={{240,0},{0,16},{16,32},{32,48},{48,64},{64,80},{80,96},{96,112},{1... | collective-permute-start | bytes 393224 | tf_op jit(solution)/shard_map/while/body/eval_jaxpr/ppermute | solution.py:15
  404.2 14.7 %collective-permute-start.1 = (bf16[256,2,128]{2,0,1:T(8,128)(2,1)S(1)}, bf16[256,2,128]{2,0,1:T(8,128)(2,1)S(1)}, u32[]{:S(2)}, u32[]{:S(2)}) collective-permute-start(bf16[256,2,128]{2,0,1:T(8,128)(2,1)S(1)} %copy.71), channel_id=1, source_target_pairs={{240,0},{0,16},{16,32},{32,48},{48,64},{64,80},{80,96},{96,112},{1... | collective-permute-start | bytes 393224 | tf_op jit(solution)/shard_map/while/body/eval_jaxpr/ppermute | solution.py:15
  419.9 15.5 %collective-permute-start.3 = (f32[256,2,128]{2,0,1:T(8,128)S(1)}, f32[256,2,128]{2,0,1:T(8,128)S(1)}, u32[]{:S(2)}, u32[]{:S(2)}) collective-permute-start(f32[256,2,128]{2,0,1:T(8,128)S(1)} %fusion.60), channel_id=1, source_target_pairs={{240,0},{0,16},{16,32},{32,48},{48,64},{64,80},{80,96},{96,112},{1... | collective-permute-start | bytes 786440 | tf_op jit(solution)/shard_map/while/body/eval_jaxpr/ppermute | solution.py:15
  420.3 15.2 %collective-permute-start.4 = (f32[256,2,128]{2,0,1:T(8,128)S(1)}, f32[256,2,128]{2,0,1:T(8,128)S(1)}, u32[]{:S(2)}, u32[]{:S(2)}) collective-permute-start(f32[256,2,128]{2,0,1:T(8,128)S(1)} %fusion.61), channel_id=1, source_target_pairs={{240,0},{0,16},{16,32},{32,48},{48,64},{64,80},{80,96},{96,112},{1... | collective-permute-start | bytes 786440 | tf_op jit(solution)/shard_map/while/body/eval_jaxpr/ppermute | solution.py:15
  420.4 15.1 %collective-permute-start = (bf16[256,2,128]{2,0,1:T(8,128)(2,1)S(1)}, bf16[256,2,128]{2,0,1:T(8,128)(2,1)S(1)}, u32[]{:S(2)}, u32[]{:S(2)}) collective-permute-start(bf16[256,2,128]{2,0,1:T(8,128)(2,1)S(1)} %copy.70), channel_id=1, source_target_pairs={{240,0},{0,16},{16,32},{32,48},{48,64},{64,80},{80,96},{96,112},{1... | collective-permute-start | bytes 393224 | tf_op jit(solution)/shard_map/while/body/eval_jaxpr/ppermute | solution.py:15
  420.5 15.0 %collective-permute-start.1 = (bf16[256,2,128]{2,0,1:T(8,128)(2,1)S(1)}, bf16[256,2,128]{2,0,1:T(8,128)(2,1)S(1)}, u32[]{:S(2)}, u32[]{:S(2)}) collective-permute-start(bf16[256,2,128]{2,0,1:T(8,128)(2,1)S(1)} %copy.71), channel_id=1, source_target_pairs={{240,0},{0,16},{16,32},{32,48},{48,64},{64,80},{80,96},{96,112},{1... | collective-permute-start | bytes 393224 | tf_op jit(solution)/shard_map/while/body/eval_jaxpr/ppermute | solution.py:15
  420.6 14.9 %collective-permute-start.2 = (s32[256]{0:T(256)S(1)}, s32[256]{0:T(256)S(1)}, u32[]{:S(2)}, u32[]{:S(2)}) collective-permute-start(s32[256]{0:T(256)S(1)} %copy.72), channel_id=1, source_target_pairs={{240,0},{0,16},{16,32},{32,48},{48,64},{64,80},{80,96},{96,112},{1... | collective-permute-start | bytes 3080 | tf_op jit(solution)/shard_map/while/body/eval_jaxpr/ppermute | solution.py:15
  436.4 15.3 %collective-permute-start.3 = (f32[256,2,128]{2,0,1:T(8,128)S(1)}, f32[256,2,128]{2,0,1:T(8,128)S(1)}, u32[]{:S(2)}, u32[]{:S(2)}) collective-permute-start(f32[256,2,128]{2,0,1:T(8,128)S(1)} %fusion.60), channel_id=1, source_target_pairs={{240,0},{0,16},{16,32},{32,48},{48,64},{64,80},{80,96},{96,112},{1... | collective-permute-start | bytes 786440 | tf_op jit(solution)/shard_map/while/body/eval_jaxpr/ppermute | solution.py:15
  436.8 14.9 %collective-permute-start.4 = (f32[256,2,128]{2,0,1:T(8,128)S(1)}, f32[256,2,128]{2,0,1:T(8,128)S(1)}, u32[]{:S(2)}, u32[]{:S(2)}) collective-permute-start(f32[256,2,128]{2,0,1:T(8,128)S(1)} %fusion.61), channel_id=1, source_target_pairs={{240,0},{0,16},{16,32},{32,48},{48,64},{64,80},{80,96},{96,112},{1... | collective-permute-start | bytes 786440 | tf_op jit(solution)/shard_map/while/body/eval_jaxpr/ppermute | solution.py:15
  436.9 14.8 %collective-permute-start = (bf16[256,2,128]{2,0,1:T(8,128)(2,1)S(1)}, bf16[256,2,128]{2,0,1:T(8,128)(2,1)S(1)}, u32[]{:S(2)}, u32[]{:S(2)}) collective-permute-start(bf16[256,2,128]{2,0,1:T(8,128)(2,1)S(1)} %copy.70), channel_id=1, source_target_pairs={{240,0},{0,16},{16,32},{32,48},{48,64},{64,80},{80,96},{96,112},{1... | collective-permute-start | bytes 393224 | tf_op jit(solution)/shard_map/while/body/eval_jaxpr/ppermute | solution.py:15
  437.0 14.7 %collective-permute-start.1 = (bf16[256,2,128]{2,0,1:T(8,128)(2,1)S(1)}, bf16[256,2,128]{2,0,1:T(8,128)(2,1)S(1)}, u32[]{:S(2)}, u32[]{:S(2)}) collective-permute-start(bf16[256,2,128]{2,0,1:T(8,128)(2,1)S(1)} %copy.71), channel_id=1, source_target_pairs={{240,0},{0,16},{16,32},{32,48},{48,64},{64,80},{80,96},{96,112},{1... | collective-permute-start | bytes 393224 | tf_op jit(solution)/shard_map/while/body/eval_jaxpr/ppermute | solution.py:15
  452.7 15.2 %collective-permute-start.3 = (f32[256,2,128]{2,0,1:T(8,128)S(1)}, f32[256,2,128]{2,0,1:T(8,128)S(1)}, u32[]{:S(2)}, u32[]{:S(2)}) collective-permute-start(f32[256,2,128]{2,0,1:T(8,128)S(1)} %fusion.60), channel_id=1, source_target_pairs={{240,0},{0,16},{16,32},{32,48},{48,64},{64,80},{80,96},{96,112},{1... | collective-permute-start | bytes 786440 | tf_op jit(solution)/shard_map/while/body/eval_jaxpr/ppermute | solution.py:15
  453.1 14.8 %collective-permute-start.4 = (f32[256,2,128]{2,0,1:T(8,128)S(1)}, f32[256,2,128]{2,0,1:T(8,128)S(1)}, u32[]{:S(2)}, u32[]{:S(2)}) collective-permute-start(f32[256,2,128]{2,0,1:T(8,128)S(1)} %fusion.61), channel_id=1, source_target_pairs={{240,0},{0,16},{16,32},{32,48},{48,64},{64,80},{80,96},{96,112},{1... | collective-permute-start | bytes 786440 | tf_op jit(solution)/shard_map/while/body/eval_jaxpr/ppermute | solution.py:15
  453.1 14.7 %collective-permute-start = (bf16[256,2,128]{2,0,1:T(8,128)(2,1)S(1)}, bf16[256,2,128]{2,0,1:T(8,128)(2,1)S(1)}, u32[]{:S(2)}, u32[]{:S(2)}) collective-permute-start(bf16[256,2,128]{2,0,1:T(8,128)(2,1)S(1)} %copy.70), channel_id=1, source_target_pairs={{240,0},{0,16},{16,32},{32,48},{48,64},{64,80},{80,96},{96,112},{1... | collective-permute-start | bytes 393224 | tf_op jit(solution)/shard_map/while/body/eval_jaxpr/ppermute | solution.py:15
  468.8 15.2 %collective-permute-start.3 = (f32[256,2,128]{2,0,1:T(8,128)S(1)}, f32[256,2,128]{2,0,1:T(8,128)S(1)}, u32[]{:S(2)}, u32[]{:S(2)}) collective-permute-start(f32[256,2,128]{2,0,1:T(8,128)S(1)} %fusion.60), channel_id=1, source_target_pairs={{240,0},{0,16},{16,32},{32,48},{48,64},{64,80},{80,96},{96,112},{1... | collective-permute-start | bytes 786440 | tf_op jit(solution)/shard_map/while/body/eval_jaxpr/ppermute | solution.py:15
  469.2 14.8 %collective-permute-start.4 = (f32[256,2,128]{2,0,1:T(8,128)S(1)}, f32[256,2,128]{2,0,1:T(8,128)S(1)}, u32[]{:S(2)}, u32[]{:S(2)}) collective-permute-start(f32[256,2,128]{2,0,1:T(8,128)S(1)} %fusion.61), channel_id=1, source_target_pairs={{240,0},{0,16},{16,32},{32,48},{48,64},{64,80},{80,96},{96,112},{1... | collective-permute-start | bytes 786440 | tf_op jit(solution)/shard_map/while/body/eval_jaxpr/ppermute | solution.py:15
  469.3 14.7 %collective-permute-start = (bf16[256,2,128]{2,0,1:T(8,128)(2,1)S(1)}, bf16[256,2,128]{2,0,1:T(8,128)(2,1)S(1)}, u32[]{:S(2)}, u32[]{:S(2)}) collective-permute-start(bf16[256,2,128]{2,0,1:T(8,128)(2,1)S(1)} %copy.70), channel_id=1, source_target_pairs={{240,0},{0,16},{16,32},{32,48},{48,64},{64,80},{80,96},{96,112},{1... | collective-permute-start | bytes 393224 | tf_op jit(solution)/shard_map/while/body/eval_jaxpr/ppermute | solution.py:15
  485.0 15.2 %collective-permute-start.3 = (f32[256,2,128]{2,0,1:T(8,128)S(1)}, f32[256,2,128]{2,0,1:T(8,128)S(1)}, u32[]{:S(2)}, u32[]{:S(2)}) collective-permute-start(f32[256,2,128]{2,0,1:T(8,128)S(1)} %fusion.60), channel_id=1, source_target_pairs={{240,0},{0,16},{16,32},{32,48},{48,64},{64,80},{80,96},{96,112},{1... | collective-permute-start | bytes 786440 | tf_op jit(solution)/shard_map/while/body/eval_jaxpr/ppermute | solution.py:15
  485.4 14.8 %collective-permute-start.4 = (f32[256,2,128]{2,0,1:T(8,128)S(1)}, f32[256,2,128]{2,0,1:T(8,128)S(1)}, u32[]{:S(2)}, u32[]{:S(2)}) collective-permute-start(f32[256,2,128]{2,0,1:T(8,128)S(1)} %fusion.61), channel_id=1, source_target_pairs={{240,0},{0,16},{16,32},{32,48},{48,64},{64,80},{80,96},{96,112},{1... | collective-permute-start | bytes 786440 | tf_op jit(solution)/shard_map/while/body/eval_jaxpr/ppermute | solution.py:15
  485.4 14.7 %collective-permute-start = (bf16[256,2,128]{2,0,1:T(8,128)(2,1)S(1)}, bf16[256,2,128]{2,0,1:T(8,128)(2,1)S(1)}, u32[]{:S(2)}, u32[]{:S(2)}) collective-permute-start(bf16[256,2,128]{2,0,1:T(8,128)(2,1)S(1)} %copy.70), channel_id=1, source_target_pairs={{240,0},{0,16},{16,32},{32,48},{48,64},{64,80},{80,96},{96,112},{1... | collective-permute-start | bytes 393224 | tf_op jit(solution)/shard_map/while/body/eval_jaxpr/ppermute | solution.py:15
  501.1 15.2 %collective-permute-start.3 = (f32[256,2,128]{2,0,1:T(8,128)S(1)}, f32[256,2,128]{2,0,1:T(8,128)S(1)}, u32[]{:S(2)}, u32[]{:S(2)}) collective-permute-start(f32[256,2,128]{2,0,1:T(8,128)S(1)} %fusion.60), channel_id=1, source_target_pairs={{240,0},{0,16},{16,32},{32,48},{48,64},{64,80},{80,96},{96,112},{1... | collective-permute-start | bytes 786440 | tf_op jit(solution)/shard_map/while/body/eval_jaxpr/ppermute | solution.py:15
  501.5 14.8 %collective-permute-start.4 = (f32[256,2,128]{2,0,1:T(8,128)S(1)}, f32[256,2,128]{2,0,1:T(8,128)S(1)}, u32[]{:S(2)}, u32[]{:S(2)}) collective-permute-start(f32[256,2,128]{2,0,1:T(8,128)S(1)} %fusion.61), channel_id=1, source_target_pairs={{240,0},{0,16},{16,32},{32,48},{48,64},{64,80},{80,96},{96,112},{1... | collective-permute-start | bytes 786440 | tf_op jit(solution)/shard_map/while/body/eval_jaxpr/ppermute | solution.py:15
  501.6 14.7 %collective-permute-start = (bf16[256,2,128]{2,0,1:T(8,128)(2,1)S(1)}, bf16[256,2,128]{2,0,1:T(8,128)(2,1)S(1)}, u32[]{:S(2)}, u32[]{:S(2)}) collective-permute-start(bf16[256,2,128]{2,0,1:T(8,128)(2,1)S(1)} %copy.70), channel_id=1, source_target_pairs={{240,0},{0,16},{16,32},{32,48},{48,64},{64,80},{80,96},{96,112},{1... | collective-permute-start | bytes 393224 | tf_op jit(solution)/shard_map/while/body/eval_jaxpr/ppermute | solution.py:15
  517.3 15.2 %collective-permute-start.3 = (f32[256,2,128]{2,0,1:T(8,128)S(1)}, f32[256,2,128]{2,0,1:T(8,128)S(1)}, u32[]{:S(2)}, u32[]{:S(2)}) collective-permute-start(f32[256,2,128]{2,0,1:T(8,128)S(1)} %fusion.60), channel_id=1, source_target_pairs={{240,0},{0,16},{16,32},{32,48},{48,64},{64,80},{80,96},{96,112},{1... | collective-permute-start | bytes 786440 | tf_op jit(solution)/shard_map/while/body/eval_jaxpr/ppermute | solution.py:15
  517.6 14.8 %collective-permute-start.4 = (f32[256,2,128]{2,0,1:T(8,128)S(1)}, f32[256,2,128]{2,0,1:T(8,128)S(1)}, u32[]{:S(2)}, u32[]{:S(2)}) collective-permute-start(f32[256,2,128]{2,0,1:T(8,128)S(1)} %fusion.61), channel_id=1, source_target_pairs={{240,0},{0,16},{16,32},{32,48},{48,64},{64,80},{80,96},{96,112},{1... | collective-permute-start | bytes 786440 | tf_op jit(solution)/shard_map/while/body/eval_jaxpr/ppermute | solution.py:15
  517.7 14.7 %collective-permute-start = (bf16[256,2,128]{2,0,1:T(8,128)(2,1)S(1)}, bf16[256,2,128]{2,0,1:T(8,128)(2,1)S(1)}, u32[]{:S(2)}, u32[]{:S(2)}) collective-permute-start(bf16[256,2,128]{2,0,1:T(8,128)(2,1)S(1)} %copy.70), channel_id=1, source_target_pairs={{240,0},{0,16},{16,32},{32,48},{48,64},{64,80},{80,96},{96,112},{1... | collective-permute-start | bytes 393224 | tf_op jit(solution)/shard_map/while/body/eval_jaxpr/ppermute | solution.py:15
  533.4 15.2 %collective-permute-start.3 = (f32[256,2,128]{2,0,1:T(8,128)S(1)}, f32[256,2,128]{2,0,1:T(8,128)S(1)}, u32[]{:S(2)}, u32[]{:S(2)}) collective-permute-start(f32[256,2,128]{2,0,1:T(8,128)S(1)} %fusion.60), channel_id=1, source_target_pairs={{240,0},{0,16},{16,32},{32,48},{48,64},{64,80},{80,96},{96,112},{1... | collective-permute-start | bytes 786440 | tf_op jit(solution)/shard_map/while/body/eval_jaxpr/ppermute | solution.py:15
  533.8 14.8 %collective-permute-start.4 = (f32[256,2,128]{2,0,1:T(8,128)S(1)}, f32[256,2,128]{2,0,1:T(8,128)S(1)}, u32[]{:S(2)}, u32[]{:S(2)}) collective-permute-start(f32[256,2,128]{2,0,1:T(8,128)S(1)} %fusion.61), channel_id=1, source_target_pairs={{240,0},{0,16},{16,32},{32,48},{48,64},{64,80},{80,96},{96,112},{1... | collective-permute-start | bytes 786440 | tf_op jit(solution)/shard_map/while/body/eval_jaxpr/ppermute | solution.py:15
  533.9 14.7 %collective-permute-start = (bf16[256,2,128]{2,0,1:T(8,128)(2,1)S(1)}, bf16[256,2,128]{2,0,1:T(8,128)(2,1)S(1)}, u32[]{:S(2)}, u32[]{:S(2)}) collective-permute-start(bf16[256,2,128]{2,0,1:T(8,128)(2,1)S(1)} %copy.70), channel_id=1, source_target_pairs={{240,0},{0,16},{16,32},{32,48},{48,64},{64,80},{80,96},{96,112},{1... | collective-permute-start | bytes 393224 | tf_op jit(solution)/shard_map/while/body/eval_jaxpr/ppermute | solution.py:15
  549.6 15.2 %collective-permute-start.3 = (f32[256,2,128]{2,0,1:T(8,128)S(1)}, f32[256,2,128]{2,0,1:T(8,128)S(1)}, u32[]{:S(2)}, u32[]{:S(2)}) collective-permute-start(f32[256,2,128]{2,0,1:T(8,128)S(1)} %fusion.60), channel_id=1, source_target_pairs={{240,0},{0,16},{16,32},{32,48},{48,64},{64,80},{80,96},{96,112},{1... | collective-permute-start | bytes 786440 | tf_op jit(solution)/shard_map/while/body/eval_jaxpr/ppermute | solution.py:15
  549.9 14.8 %collective-permute-start.4 = (f32[256,2,128]{2,0,1:T(8,128)S(1)}, f32[256,2,128]{2,0,1:T(8,128)S(1)}, u32[]{:S(2)}, u32[]{:S(2)}) collective-permute-start(f32[256,2,128]{2,0,1:T(8,128)S(1)} %fusion.61), channel_id=1, source_target_pairs={{240,0},{0,16},{16,32},{32,48},{48,64},{64,80},{80,96},{96,112},{1... | collective-permute-start | bytes 786440 | tf_op jit(solution)/shard_map/while/body/eval_jaxpr/ppermute | solution.py:15
  550.0 14.7 %collective-permute-start = (bf16[256,2,128]{2,0,1:T(8,128)(2,1)S(1)}, bf16[256,2,128]{2,0,1:T(8,128)(2,1)S(1)}, u32[]{:S(2)}, u32[]{:S(2)}) collective-permute-start(bf16[256,2,128]{2,0,1:T(8,128)(2,1)S(1)} %copy.70), channel_id=1, source_target_pairs={{240,0},{0,16},{16,32},{32,48},{48,64},{64,80},{80,96},{96,112},{1... | collective-permute-start | bytes 393224 | tf_op jit(solution)/shard_map/while/body/eval_jaxpr/ppermute | solution.py:15
  565.7 15.2 %collective-permute-start.3 = (f32[256,2,128]{2,0,1:T(8,128)S(1)}, f32[256,2,128]{2,0,1:T(8,128)S(1)}, u32[]{:S(2)}, u32[]{:S(2)}) collective-permute-start(f32[256,2,128]{2,0,1:T(8,128)S(1)} %fusion.60), channel_id=1, source_target_pairs={{240,0},{0,16},{16,32},{32,48},{48,64},{64,80},{80,96},{96,112},{1... | collective-permute-start | bytes 786440 | tf_op jit(solution)/shard_map/while/body/eval_jaxpr/ppermute | solution.py:15
  566.1 14.8 %collective-permute-start.4 = (f32[256,2,128]{2,0,1:T(8,128)S(1)}, f32[256,2,128]{2,0,1:T(8,128)S(1)}, u32[]{:S(2)}, u32[]{:S(2)}) collective-permute-start(f32[256,2,128]{2,0,1:T(8,128)S(1)} %fusion.61), channel_id=1, source_target_pairs={{240,0},{0,16},{16,32},{32,48},{48,64},{64,80},{80,96},{96,112},{1... | collective-permute-start | bytes 786440 | tf_op jit(solution)/shard_map/while/body/eval_jaxpr/ppermute | solution.py:15
  566.2 14.7 %collective-permute-start = (bf16[256,2,128]{2,0,1:T(8,128)(2,1)S(1)}, bf16[256,2,128]{2,0,1:T(8,128)(2,1)S(1)}, u32[]{:S(2)}, u32[]{:S(2)}) collective-permute-start(bf16[256,2,128]{2,0,1:T(8,128)(2,1)S(1)} %copy.70), channel_id=1, source_target_pairs={{240,0},{0,16},{16,32},{32,48},{48,64},{64,80},{80,96},{96,112},{1... | collective-permute-start | bytes 393224 | tf_op jit(solution)/shard_map/while/body/eval_jaxpr/ppermute | solution.py:15
  (29 other events, 339.2 us)
Sparse Core Ops, SparseCore 0:
  10.8 53.0 all-gather.7
  67.0 50.8 all-gather.5
  120.7 52.4 all-gather.9
  174.8 77.9 all-gather.11
  264.1 75.5 reduce-scatter.2
  344.5 109.5 reduce-scatter.4
where the time goes:
time: 592 us
  waiting for transfers between devices  484 us (82%)
  matrix products  39.8 us (7%)
  blocking collectives  22.1 us (4%)
  between operations  14.3 us (2%)
  local copies, waits for them, and re-layouts  12.1 us (2%)
  starting transfers between devices  9.97 us (2%)
  other arithmetic  6.96 us (1%)
    ppermute x80, waiting for transfers between devices, shifted(): return lax.ppermute(block, axis, route)  276 us
    all_gather x1, waiting for transfers between devices, shards(): cotangent_full = lax.all_gather(cotangent, 'fsdp', axis=1, tiled=True)  79.6 us
    all_gather x1, waiting for transfers between devices, shards(): piece_keys = lax.all_gather(key_states, 'seq', axis=0, tiled=True)  51.1 us
    all_gather x1, waiting for transfers between devices, shards(): weight_full = lax.all_gather(out_weight, 'seq', axis=1, tiled=True)  47.9 us
    all_gather x1, waiting for transfers between devices, shards(): piece_values = lax.all_gather(value_states, 'seq', axis=0, tiled=True)  27.4 us
    all_gather x1, blocking collectives, shards(): piece_pos = lax.all_gather(positions, 'seq', axis=0, tiled=True)  22.1 us
  transfers between devices with their start and end apart: 86, of which 20 were waited for; matrix products, arithmetic and copies ran while one was open for 8% of the time, Pallas kernels for 0%

commit v1 on v0

v1 whole, which is shorter than its diff:
```python
import math

import jax
import jax.numpy as jnp
from jax import lax
from jax.experimental import pallas as pl
from jax.experimental.pallas import tpu as pltpu
from jax.sharding import PartitionSpec as P

HEAD_DIM = 128
TOKENS = 256
HALF = 128
COLS = 320
FEATS = 256
MESH = pl.DeviceIdType.MESH
BF16 = jnp.bfloat16
F32 = jnp.float32
SCALE = HEAD_DIM ** (-0.5)
SCALE_LOG2 = SCALE * math.log2(math.e)
BLOCKED = -1e30
SEMS = 80


def mm(a, b):
    return jnp.dot(a, b, preferred_element_type=F32)


def mm_nt(a, b):
    return lax.dot_general(a, b, (((1,), (1,)), ((), ())), preferred_element_type=F32)


def mm_tn(a, b):
    return lax.dot_general(a, b, (((0,), (0,)), ((), ())), preferred_element_type=F32)


def kernel(
    q_ref, k_ref, v_ref, res_ref, w_ref, ct_ref,
    out_ref, dq_ref, dk_ref, dv_ref, gw_ref,
    kvr, kvp, qt, qp, wt, cot,
    m_ref, l_ref, acc, att_t, att, att_full,
    pga, pga_in, grad_t, grad, delta,
    out_send, out_rin, out_lin, out_pair_ici, out_pair_core,
    gw_send, gw_rin2, gw_lin2, gw_rin, gw_lin, gw_x, gw_own,
    df, d_send, d_rin2, d_lin2, d_rin, d_lin, d_x, fin, fin_in,
    dq_t, dq_b, dq_in,
    ss, rs,
):
    seq = lax.axis_index("seq")
    fsdp = lax.axis_index("fsdp")
    xh, y, c = seq // 8, (seq // 2) % 4, seq % 2
    z, xl = fsdp // 2, fsdp % 2
    p = 1 - c
    same = c == xl

    def dev(xh_, y_, c_, z_, xl_):
        return (xh_ * 8 + y_ * 2 + c_, z_ * 2 + xl_)

    yr, yl, y2 = (y + 1) % 4, (y + 3) % 4, (y + 2) % 4
    zr, zl = (z + 1) % 8, (z + 7) % 8
    core_peer = dev(xh, y, p, z, xl)
    xh_peer = dev(1 - xh, y, c, z, xl)
    y_right, y_left = dev(xh, yr, c, z, xl), dev(xh, yl, c, z, xl)
    z_right, z_left = dev(xh, y, c, zr, xl), dev(xh, y, c, zl, xl)
    xl_peers = [dev(xh, y, h, z, 1 - xl) for h in range(2)]
    xl_owner = dev(xh, y, xl, z, 1 - xl)

    used = [0]
    sent = []

    def take(count=1):
        first = used[0]
        used[0] += count
        return first

    def copy(src, dst, to):
        i = take()
        d = pltpu.make_async_remote_copy(
            src_ref=src, dst_ref=dst, send_sem=ss.at[i], recv_sem=rs.at[i],
            device_id=to, device_id_type=MESH,
        )
        d.start()
        sent.append(d)
        return d

    barrier = pltpu.get_barrier_semaphore()
    peers = [core_peer, xh_peer, y_right, y_left, z_right, z_left] + xl_peers
    for peer in peers:
        pl.semaphore_signal(barrier, inc=1, device_id=peer, device_id_type=MESH)
    pl.semaphore_wait(barrier, len(peers))

    sem_ici, sem_core = take(2), take()
    cot_ici = pltpu.make_async_remote_copy(
        src_ref=ct_ref, dst_ref=cot.at[z, c], send_sem=ss.at[sem_ici], recv_sem=rs.at[sem_ici + c],
        device_id=xl_owner, device_id_type=MESH,
    )
    cot_ici.start()
    sent.append(cot_ici)
    cot_core = pltpu.make_async_remote_copy(
        src_ref=ct_ref, dst_ref=cot.at[z, c], send_sem=ss.at[sem_core], recv_sem=rs.at[sem_core],
        device_id=core_peer, device_id_type=MESH,
    )

    @pl.when(jnp.logical_not(same))
    def _():
        cot_core.start()

    first = c == 0
    own = y * 4 + xh * 2
    for part, ref in ((0, k_ref), (1, v_ref)):
        lo, hi = ref[:, :HEAD_DIM], ref[:, HEAD_DIM:]
        rows = pl.ds(part * TOKENS, TOKENS)
        kvp[rows, :] = jnp.where(first, hi, lo)
        kvr[own + c, rows, :] = jnp.where(first, lo, hi)
    kvp[pl.ds(2 * TOKENS, 16), :] = res_ref[...]
    kvr[own + c, pl.ds(2 * TOKENS, 16), :] = res_ref[...]
    kv_core = copy(kvp, kvr.at[own + c], core_peer)
    for i in range(2):
        rows = pl.ds(i * HALF, HALF)
        lo, hi = q_ref[rows, :HEAD_DIM], q_ref[rows, HEAD_DIM:]
        qp[i] = jnp.where(first, hi, lo)
        qt[i, c] = jnp.where(first, lo, hi)
    q_core = copy(qp, qt.at[:, c], core_peer)

    w_own = y * 2 + xh
    wt[w_own] = w_ref[...]

    @pl.when(same)
    def _():
        cot[z, c] = ct_ref[...]

    acc[...] = jnp.zeros_like(acc)
    l_ref[...] = jnp.zeros_like(l_ref)
    m_ref[...] = jnp.full_like(m_ref, BLOCKED)

    kv_core.wait_recv()

    def kv_direct(x):
        block = kvr.at[pl.ds(y * 4 + x * 2, 2)]
        return copy(block, block, y_right), copy(block, block, y_left)

    def kv_forward(x):
        low, high = kvr.at[yl * 4 + x * 2], kvr.at[yr * 4 + x * 2 + 1]
        return copy(low, low, y_right), copy(high, high, y_left)

    def w_direct(x):
        block = wt.at[y * 2 + x]
        return copy(block, block, y_right), copy(block, block, y_left)

    def w_forward(x):
        low, high = wt.at[yl * 2 + x, pl.ds(0, 160)], wt.at[yr * 2 + x, pl.ds(160, 160)]
        return copy(low, low, y_right), copy(high, high, y_left)

    def both_recv(pair):
        pair[0].wait_recv()
        pair[1].wait_recv()

    kv_xh = copy(kvr.at[pl.ds(own, 2)], kvr.at[pl.ds(own, 2)], xh_peer)
    kv_mine = kv_direct(xh)

    @pl.when(same)
    def _():
        cot_core.wait_recv()

    @pl.when(jnp.logical_not(same))
    def _():
        for h in range(2):
            pltpu.make_async_remote_copy(
                src_ref=ct_ref, dst_ref=cot.at[z, h], send_sem=ss.at[sem_ici],
                recv_sem=rs.at[sem_ici + h], device_id=xl_owner, device_id_type=MESH,
            ).wait_recv()

    def z_pair(right_slot, left_slot):
        a, b = cot.at[right_slot], cot.at[left_slot]
        return copy(a, a, z_right), copy(b, b, z_left)

    z_one = z_pair(z, z)
    w_xh = copy(wt.at[w_own], wt.at[w_own], xh_peer)
    q_core.wait_recv()

    kv_xh.wait_recv()
    kv_other = kv_direct(1 - xh)
    both_recv(kv_mine)
    kv_mine_far = kv_forward(xh)
    both_recv(z_one)
    z_two = z_pair((z + 7) % 8, (z + 1) % 8)
    w_mine = w_direct(xh)

    ahead = (
        lax.broadcasted_iota(jnp.int32, (1, HALF, TOKENS), 2) % HALF
        - lax.broadcasted_iota(jnp.int32, (1, HALF, TOKENS), 1)
    )

    def residue_rows(slot, count):
        return kvr[pl.ds(slot, count), pl.ds(2 * TOKENS, 16), :].astype(F32)[:, 0:1, :]

    query_res = residue_rows(own, 2)
    query_res = jnp.concatenate([query_res[0:1], query_res[1:2]], axis=2)

    def tile_scores(yy, t, qi, ki):
        key_res = residue_rows(yy * 4, 4)
        key_res = jnp.concatenate([key_res, key_res], axis=2)
        bound = jnp.where(key_res <= query_res, 0, 1) - jnp.where(qi > ki, 4 * HALF, 0)
        rows = pl.multiple_of(ki * HALF, HALF)
        keys = kvr[pl.ds(yy * 4, 4), pl.ds(rows, HALF), :].reshape(4 * HALF, HEAD_DIM)
        values = kvr[pl.ds(yy * 4, 4), pl.ds(TOKENS + rows, HALF), :].reshape(4 * HALF, HEAD_DIM)
        queries = qt[qi].reshape(TOKENS, HEAD_DIM)
        scores = mm_nt(keys, queries) * SCALE_LOG2
        seen = ahead >= bound
        scores = jnp.where(seen, scores.reshape(4, HALF, TOKENS), BLOCKED)
        return scores.reshape(4 * HALF, TOKENS), keys, values, queries

    def forward(yy):
        def tile(t, carry):
            qi, ki = (t + 1) // 2, t // 2
            scores, _, values, _ = tile_scores(yy, t, qi, ki)
            old = m_ref[qi]
            new = jnp.maximum(old, jnp.max(scores, axis=0, keepdims=True))
            probs = jnp.exp2(scores - new)
            shrink = jnp.exp2(old - new)
            m_ref[qi] = new
            l_ref[qi] = l_ref[qi] * shrink + jnp.sum(probs, axis=0, keepdims=True)
            acc[qi] = acc[qi] * shrink + mm_tn(values, probs.astype(BF16))
            return carry

        lax.fori_loop(0, 3, tile, 0)

    forward(y)
    w_xh.wait_recv()
    w_other = w_direct(1 - xh)
    both_recv(kv_other)
    kv_other_far = kv_forward(1 - xh)
    both_recv(z_two)
    z_three = z_pair((z + 6) % 8, (z + 2) % 8)
    forward(yl)
    forward(yr)
    both_recv(w_mine)
    w_mine_far = w_forward(xh)
    both_recv(z_three)
    z_four = (
        copy(cot.at[(z + 5) % 8, 0], cot.at[(z + 5) % 8, 0], z_right),
        copy(cot.at[(z + 3) % 8, 1], cot.at[(z + 3) % 8, 1], z_left),
    )
    both_recv(w_other)
    w_other_far = w_forward(1 - xh)
    both_recv(kv_mine_far)
    both_recv(kv_other_far)
    forward(y2)

    for qi in range(2):
        total = l_ref[qi]
        rows = (acc[qi] / total).astype(BF16)
        att_t[qi] = rows
        m_ref[qi] = m_ref[qi] + jnp.log2(total)
        wide = rows.astype(F32)
        for h in range(2):
            att[c, h, pl.ds(qi * HALF, HALF), :] = wide[:, h * HALF:(h + 1) * HALF].T.astype(BF16)
    att_core = copy(att.at[c], att.at[c], core_peer)
    both_recv(w_mine_far)
    both_recv(w_other_far)
    att_core.wait_recv()
    for h in range(2):
        att_full[h] = jnp.concatenate([att[0, h], att[1, h]], axis=1)

    def w_block(i):
        return wt[(i % 4) * 2 + i // 4]

    def out_term(i, h):
        return mm_nt(w_block(i), att_full[h])

    def out_step(step, got):
        to_right, to_left = (z + 4 - step) % 8, (z + 4 + step) % 8
        if step == 0:
            out_send[0, 0, 0] = out_term(to_right, 0).astype(BF16)
            out_send[1, 0, 1] = out_term(to_left, 1).astype(BF16)
            return (
                copy(out_send.at[0, 0, 0], out_rin.at[0, 0], z_right),
                copy(out_send.at[1, 0, 1], out_lin.at[0, 1], z_left),
            )
        both_recv(got)
        for side, target, arrived in ((0, to_right, out_rin), (1, to_left, out_lin)):
            for h in range(2):
                term = out_term(target, h)
                if step > 1 or h == side:
                    term = term + arrived[step - 1, h].astype(F32)
                out_send[side, step, h] = term.astype(BF16)
        return (
            copy(out_send.at[0, step], out_rin.at[step], z_right),
            copy(out_send.at[1, step], out_lin.at[step], z_left),
        )

    out_0 = out_step(0, None)
    both_recv(z_four)

    pga[...] = jnp.zeros_like(pga)

    def width_step(i, carry):
        weight = w_block(i)
        for h in range(2):
            term = mm_tn(weight, cot[i, h])
            pga[0, h] += term[:HEAD_DIM]
            pga[1, h] += term[HEAD_DIM:]
        return carry

    lax.fori_loop(0, 8, width_step, 0)
    pga_core = copy(pga.at[p], pga_in, core_peer)

    def gw_term(x, yy):
        i = x * 4 + yy
        return mm(cot[i, 0], att_full[0]) + mm(cot[i, 1], att_full[1])

    for x in range(2):
        gw_send[0, x] = gw_term(x, y2).astype(BF16)
    gw_far = (copy(gw_send.at[0, 0], gw_rin2, y_right), copy(gw_send.at[0, 1], gw_lin2, y_left))

    pga_core.wait_recv()
    for h in range(2):
        rows = (pga[c, h] + pga_in[h]).astype(BF16)
        for qi in range(2):
            grad_t[qi, :, h * HALF:(h + 1) * HALF] = rows[:, qi * HALF:(qi + 1) * HALF]
    for qi in range(2):
        wide = grad_t[qi].astype(F32)
        delta[qi] = jnp.sum(wide * att_t[qi].astype(F32), axis=0, keepdims=True)
        grad[qi] = wide.T.astype(BF16)
    dq_t[...] = jnp.zeros_like(dq_t)

    def backward(yy):
        df[...] = jnp.zeros_like(df)

        def tile(t, carry):
            qi, ki = (t + 1) // 2, t // 2
            scores, keys, values, queries = tile_scores(yy, t, qi, ki)
            probs = jnp.exp2(scores - m_ref[qi])
            grad_probs = mm(values, grad_t[qi])
            grad_scores = (probs * (grad_probs - delta[qi])).astype(BF16)
            rows = pl.ds(pl.multiple_of(ki * HALF, HALF), HALF)
            grad_keys = mm(grad_scores, queries).reshape(4, HALF, HEAD_DIM)
            grad_values = mm(probs.astype(BF16), grad[qi]).reshape(4, HALF, HEAD_DIM)
            df[:, 0, rows, :] += grad_keys
            df[:, 1, rows, :] += grad_values
            dq_t[qi] += mm_tn(keys, grad_scores)
            return carry

        lax.fori_loop(0, 3, tile, 0)

    backward(y2)
    for x in range(2):
        d_send[0, pl.ds(2 * x, 2)] = df[pl.ds(2 * x, 2)].astype(BF16)
    d_far = (
        copy(d_send.at[0, pl.ds(0, 2)], d_rin2, y_right),
        copy(d_send.at[0, pl.ds(2, 2)], d_lin2, y_left),
    )
    out_1 = out_step(1, out_0)

    both_recv(gw_far)
    gw_send[1, 0] = (gw_term(0, yr) + gw_rin2[...].astype(F32)).astype(BF16)
    gw_send[1, 1] = gw_term(1, yr).astype(BF16)
    gw_send[2, 0] = gw_term(0, yl).astype(BF16)
    gw_send[2, 1] = (gw_term(1, yl) + gw_lin2[...].astype(F32)).astype(BF16)

    backward(yr)
    both_recv(d_far)
    d_send[1, pl.ds(0, 2)] = (df[pl.ds(0, 2)] + d_rin2[...].astype(F32)).astype(BF16)
    d_send[1, pl.ds(2, 2)] = df[pl.ds(2, 2)].astype(BF16)
    d_right = copy(d_send.at[1], d_rin, y_right)
    backward(yl)
    d_send[2, pl.ds(0, 2)] = df[pl.ds(0, 2)].astype(BF16)
    d_send[2, pl.ds(2, 2)] = (df[pl.ds(2, 2)] + d_lin2[...].astype(F32)).astype(BF16)
    d_left = copy(d_send.at[2], d_lin, y_left)
    gw_near = (copy(gw_send.at[1], gw_rin, y_right), copy(gw_send.at[2], gw_lin, y_left))
    out_2 = out_step(2, out_1)

    backward(y)
    for qi in range(2):
        for h in range(2):
            dq_b[h, pl.ds(qi * HALF, HALF), :] = dq_t[qi, :, h * HALF:(h + 1) * HALF].T * SCALE
    dq_core = copy(dq_b.at[p], dq_in, core_peer)
    out_3 = out_step(3, out_2)

    d_right.wait_recv()
    d_left.wait_recv()
    d_send[3, pl.ds(0, 2)] = (
        df[pl.ds(2 * (1 - xh), 2)]
        + d_rin[pl.ds(2 * (1 - xh), 2)].astype(F32)
        + d_lin[pl.ds(2 * (1 - xh), 2)].astype(F32)
    ).astype(BF16)
    d_over = copy(d_send.at[3, pl.ds(0, 2)], d_x, xh_peer)

    both_recv(gw_near)
    for x in range(2):
        gw_own[x] = gw_term(x, y) + gw_rin[x].astype(F32) + gw_lin[x].astype(F32)
    gw_send[3, 0] = gw_own[1 - xh].astype(BF16)
    gw_over = copy(gw_send.at[3, 0], gw_x, xh_peer)

    def place(ref, mine, theirs):
        ref[:, :HEAD_DIM] = jnp.where(first, mine, theirs)
        ref[:, HEAD_DIM:] = jnp.where(first, theirs, mine)

    dq_core.wait_recv()
    place(dq_ref, dq_b[c], dq_in[...])

    d_over.wait_recv()
    for part in range(2):
        total = (
            df[pl.ds(2 * xh, 2), part]
            + d_rin[pl.ds(2 * xh, 2), part].astype(F32)
            + d_lin[pl.ds(2 * xh, 2), part].astype(F32)
            + d_x[:, part].astype(F32)
        )
        fin[:, part] = total * SCALE if part == 0 else total
    fin_core = copy(fin.at[p], fin_in, core_peer)

    both_recv(out_3)
    for h in range(2):
        term = out_term(z, h) + out_rin[3, h].astype(F32) + out_lin[3, h].astype(F32)
        out_send[0, 4, h] = term.astype(BF16)
    pair_ici, pair_core = take(2), take()
    to_peers = [
        pltpu.make_async_remote_copy(
            src_ref=out_send.at[0, 4, h], dst_ref=out_pair_ici, send_sem=ss.at[pair_ici + h],
            recv_sem=rs.at[pair_ici], device_id=xl_peers[h], device_id_type=MESH,
        )
        for h in range(2)
    ]
    to_core = pltpu.make_async_remote_copy(
        src_ref=out_send.at[0, 4, p], dst_ref=out_pair_core, send_sem=ss.at[pair_core],
        recv_sem=rs.at[pair_core], device_id=core_peer, device_id_type=MESH,
    )

    @pl.when(same)
    def _():
        to_core.start()

    @pl.when(jnp.logical_not(same))
    def _():
        to_peers[0].start()
        to_peers[1].start()

    gw_over.wait_recv()
    gw_ref[...] = gw_own[xh] + gw_x[...].astype(F32)

    fin_core.wait_recv()
    place(dk_ref, fin[c, 0], fin_in[0])
    place(dv_ref, fin[c, 1], fin_in[1])

    to_peers[0].wait_recv()

    @pl.when(same)
    def _():
        out_ref[...] = out_send[0, 4, c].astype(F32) + out_pair_ici[...].astype(F32)
        to_core.wait_send()

    @pl.when(jnp.logical_not(same))
    def _():
        to_core.wait_recv()
        out_ref[...] = out_pair_core[...].astype(F32) + out_pair_ici[...].astype(F32)
        to_peers[0].wait_send()
        to_peers[1].wait_send()
        cot_core.wait_send()

    for d in sent:
        d.wait_send()
    assert used[0] <= SEMS, used[0]


def fused(q, k, v, res, w, ct):
    vm = pltpu.VMEM
    scratch = [
        vm((16, 2 * TOKENS + 16, HEAD_DIM), BF16),
        vm((2 * TOKENS + 16, HEAD_DIM), BF16),
        vm((2, 2, HALF, HEAD_DIM), BF16),
        vm((2, HALF, HEAD_DIM), BF16),
        vm((8, COLS, FEATS), BF16),
        vm((8, 2, COLS, TOKENS), BF16),
        vm((2, 1, TOKENS), F32),
        vm((2, 1, TOKENS), F32),
        vm((2, HEAD_DIM, TOKENS), F32),
        vm((2, HEAD_DIM, TOKENS), BF16),
        vm((2, 2, TOKENS, HEAD_DIM), BF16),
        vm((2, TOKENS, FEATS), BF16),
        vm((2, 2, HEAD_DIM, TOKENS), F32),
        vm((2, HEAD_DIM, TOKENS), F32),
        vm((2, HEAD_DIM, TOKENS), BF16),
        vm((2, TOKENS, HEAD_DIM), BF16),
        vm((2, 1, TOKENS), F32),
        vm((2, 5, 2, COLS, TOKENS), BF16),
        vm((4, 2, COLS, TOKENS), BF16),
        vm((4, 2, COLS, TOKENS), BF16),
        vm((COLS, TOKENS), BF16),
        vm((COLS, TOKENS), BF16),
        vm((4, 2, COLS, FEATS), BF16),
        vm((COLS, FEATS), BF16),
        vm((COLS, FEATS), BF16),
        vm((2, COLS, FEATS), BF16),
        vm((2, COLS, FEATS), BF16),
        vm((COLS, FEATS), BF16),
        vm((2, COLS, FEATS), F32),
        vm((4, 2, TOKENS, HEAD_DIM), F32),
        vm((4, 4, 2, TOKENS, HEAD_DIM), BF16),
        vm((2, 2, TOKENS, HEAD_DIM), BF16),
        vm((2, 2, TOKENS, HEAD_DIM), BF16),
        vm((4, 2, TOKENS, HEAD_DIM), BF16),
        vm((4, 2, TOKENS, HEAD_DIM), BF16),
        vm((2, 2, TOKENS, HEAD_DIM), BF16),
        vm((2, 2, TOKENS, HEAD_DIM), F32),
        vm((2, TOKENS, HEAD_DIM), F32),
        vm((2, HEAD_DIM, TOKENS), F32),
        vm((2, TOKENS, HEAD_DIM), F32),
        vm((TOKENS, HEAD_DIM), F32),
        pltpu.SemaphoreType.DMA((SEMS,)),
        pltpu.SemaphoreType.DMA((SEMS,)),
    ]
    whole = pl.BlockSpec(memory_space=pltpu.VMEM)
    shape = jax.ShapeDtypeStruct
    return pl.pallas_call(
        kernel,
        name="attention_core",
        out_shape=(
            shape((COLS, TOKENS), F32),
            shape((TOKENS, FEATS), F32),
            shape((TOKENS, FEATS), F32),
            shape((TOKENS, FEATS), F32),
            shape((COLS, FEATS), F32),
        ),
        in_specs=[whole] * 6,
        out_specs=(whole,) * 5,
        scratch_shapes=scratch,
        compiler_params=pltpu.CompilerParams(
            collective_id=0, has_side_effects=True, vmem_limit_bytes=48 << 20
        ),
    )(q, k, v, res, w, ct)


def shards(query_states, key_states, value_states, positions, out_weight, cotangent):
    blocks = lax.axis_size("seq")
    residue = jnp.broadcast_to((positions[0] % blocks).astype(BF16), (16, HEAD_DIM))
    out_t, grad_queries, grad_keys, grad_values, gw_t = fused(
        query_states, key_states, value_states, residue, out_weight.T, cotangent.T
    )
    return out_t.T, grad_queries, grad_keys, grad_values, gw_t.T


def solution(mesh):
    in_specs = (
        P("seq", "fsdp"),
        P("seq", "fsdp"),
        P("seq", "fsdp"),
        P("seq"),
        P("fsdp", "seq"),
        P("seq", "fsdp"),
    )
    out_specs = (
        P("seq", "fsdp"),
        P("seq", "fsdp"),
        P("seq", "fsdp"),
        P("seq", "fsdp"),
        P("fsdp", "seq"),
    )
    return jax.shard_map(shards, mesh=mesh, in_specs=in_specs, out_specs=out_specs, check_vma=False)
```

time: 592 us -> 103 us (0.17)
  the two profiles are of different devices: /device:TPU:4 before, /device:TPU:1 now
where the time goes in v1:
time: 103 us
  Pallas kernels  90.8 us (88%)
  local copies, waits for them, and re-layouts  9.28 us (9%)
  between operations  2.63 us (3%)
    pallas_call x1, Pallas kernels, fused(): pl.pallas_call(kernel, name='attention_core', out_shape=(shape((COLS, TOK...  90.8 us
    unnamed x17, local copies, waits for them, and re-layouts  8.77 us

profile of v1, /device:TPU:1, one launch (start us, length us, event | category | flops | bytes accessed | tf_op | source)
XLA Modules:
  0.0 102.7 jit_solution(14155095573730763833)
XLA Ops:
  0.6 0.0 copy-start.5
  0.6 0.7 copy-done.5
  1.3 0.5 slice.3
  3.8 0.0 copy-start
  3.8 0.9 copy-done
  4.7 0.0 copy-start.1
  4.7 0.9 copy-done.1
  5.6 0.0 copy-start.2
  5.6 0.9 copy-done.2
  6.5 0.0 copy-start.3
  6.5 0.9 copy-done.3
  7.4 0.0 copy-start.4
  7.4 0.9 copy-done.4
  8.3 90.8 %attention_core.1 = (f32[320,256]{1,0:T(8,128)S(1)}, f32[256,256]{1,0:T(8,128)S(1)}, f32[256,256]{1,0:T(8,128)S(1)}, f32[256,256]{1,0:T(8,128)S(1)}, f32[320,256]{1,0:T(8,128)S(1)}) custom-call(bf16[256,256]{1,0:T(8,128)(2,1)S(1)} %copy-done.2, bf16[256,256]{1,0:T(8,128)(2,1)S(1)} %copy-done.3, bf16[256,256]{1,0:T(8,128)(2,1)S(1)} %copy-done.4, ...), custom_call_target="tpu_custom_call" | custom-call | tf_op jit(solution)/shard_map/attention_core/pallas_call | solution.py:514
  99.1 0.7 copy.16
  99.9 0.7 copy.17
  100.6 0.7 copy.18
  101.3 0.7 copy.19
  102.0 0.7 copy.20
  (1 shorter events, 0.0 us)
Async XLA Ops:
  0.6 0.7 copy-start.5
  3.8 0.9 copy-start
  4.7 0.9 copy-start.1
  5.6 0.9 copy-start.2
  6.5 0.9 copy-start.3
  7.4 0.9 copy-start.4

commit v2 on v1

v2 whole, which is shorter than its diff:
```python
import math

import jax
import jax.numpy as jnp
from jax import lax
from jax.experimental import pallas as pl
from jax.experimental.pallas import tpu as pltpu
from jax.sharding import PartitionSpec as P

HEAD_DIM = 128
TOKENS = 256
HALF = 128
COLS = 320
FEATS = 256
MESH = pl.DeviceIdType.MESH
BF16 = jnp.bfloat16
F32 = jnp.float32
SCALE = HEAD_DIM ** (-0.5)
SCALE_LOG2 = SCALE * math.log2(math.e)
BLOCKED = -1e30
SEMS = 100


def mm(a, b):
    return jnp.dot(a, b, preferred_element_type=F32)


def mm_nt(a, b):
    return lax.dot_general(a, b, (((1,), (1,)), ((), ())), preferred_element_type=F32)


def mm_tn(a, b):
    return lax.dot_general(a, b, (((0,), (0,)), ((), ())), preferred_element_type=F32)


def kernel(
    pos_ref, q_ref, k_ref, v_ref, w_ref, ct_ref,
    out_hbm, dq_hbm, dk_hbm, dv_hbm, gw_hbm,
    out_ref, dq_ref, dk_ref, dv_ref, gw_ref,
    kvr, res, qt, wt, cot,
    m_ref, l_ref, acc, att_t, att, att_full,
    pga, pga_in, grad_t, grad, delta,
    out_send, out_in, out_fin, out_pair_ici, out_pair_core,
    gw_xsend, gw_xin, gw_send, gw_rin2, gw_lin2, gw_rin, gw_lin,
    df, d_send, d_rin2, d_lin2, d_rin, d_lin, d_x, fin, fin_in,
    dq_t, dq_b, dq_in,
    ss, rs, ls,
):
    seq = lax.axis_index("seq")
    fsdp = lax.axis_index("fsdp")
    xh, y, c = seq // 8, (seq // 2) % 4, seq % 2
    z, xl = fsdp // 2, fsdp % 2
    p = 1 - c
    same = c == xl

    def dev(xh_, y_, c_, z_, xl_):
        return (xh_ * 8 + y_ * 2 + c_, z_ * 2 + xl_)

    yr, yl, y2 = (y + 1) % 4, (y + 3) % 4, (y + 2) % 4
    zr, zl = (z + 1) % 8, (z + 7) % 8
    core_peer = dev(xh, y, p, z, xl)
    xh_peer = dev(1 - xh, y, c, z, xl)
    y_right, y_left = dev(xh, yr, c, z, xl), dev(xh, yl, c, z, xl)
    z_right, z_left = dev(xh, y, c, zr, xl), dev(xh, y, c, zl, xl)
    xl_peers = [dev(xh, y, h, z, 1 - xl) for h in range(2)]
    xl_owner = dev(xh, y, xl, z, 1 - xl)

    used = [0]
    sent = []

    def take(count=1):
        first = used[0]
        used[0] += count
        return first

    def copy(src, dst, to):
        i = take()
        d = pltpu.make_async_remote_copy(
            src_ref=src, dst_ref=dst, send_sem=ss.at[i], recv_sem=rs.at[i],
            device_id=to, device_id_type=MESH,
        )
        d.start()
        sent.append(d)
        return d

    stores = []

    def store(i, src, dst):
        d = pltpu.make_async_copy(src, dst, ls.at[5 + i])
        d.start()
        stores.append(d)

    def arrived(*copies):
        for d in copies:
            d.wait_recv()

    own = y * 4 + xh * 2
    w_own = y * 2 + xh
    mine = pl.ds(pl.multiple_of(c * HEAD_DIM, HEAD_DIM), HEAD_DIM)
    other = pl.ds(pl.multiple_of(p * HEAD_DIM, HEAD_DIM), HEAD_DIM)
    key_rows, value_rows, res_rows = pl.ds(0, TOKENS), pl.ds(TOKENS, TOKENS), pl.ds(2 * TOKENS, 16)
    key_copy = pltpu.make_async_copy(k_ref.at[:, mine], kvr.at[own + c, key_rows], ls.at[0])
    value_copy = pltpu.make_async_copy(v_ref.at[:, mine], kvr.at[own + c, value_rows], ls.at[1])
    query_copy = pltpu.make_async_copy(q_ref.at[:, mine], qt.at[c], ls.at[2])
    weight_copy = pltpu.make_async_copy(w_ref, wt.at[w_own], ls.at[3])
    cot_copy = pltpu.make_async_copy(ct_ref, cot.at[z, c], ls.at[4])
    key_copy.start()
    value_copy.start()

    @pl.when(same)
    def _():
        cot_copy.start()

    query_copy.start()
    weight_copy.start()

    barrier = pltpu.get_barrier_semaphore()
    peers = [core_peer, xh_peer, y_right, y_left, z_right, z_left] + xl_peers
    for peer in peers:
        pl.semaphore_signal(barrier, inc=1, device_id=peer, device_id_type=MESH)
    residue = jnp.full((16, HEAD_DIM), (pos_ref[0] % 16).astype(F32)).astype(BF16)
    res[...] = residue
    kvr[own + c, res_rows, :] = residue
    pl.semaphore_wait(barrier, len(peers))

    core_first = (
        copy(k_ref.at[:, other], kvr.at[own + c, key_rows], core_peer),
        copy(v_ref.at[:, other], kvr.at[own + c, value_rows], core_peer),
        copy(res, kvr.at[own + c, res_rows], core_peer),
    )

    sem_ici, sem_core = take(2), take()
    cot_ici = pltpu.make_async_remote_copy(
        src_ref=ct_ref, dst_ref=cot.at[z, c], send_sem=ss.at[sem_ici], recv_sem=rs.at[sem_ici + c],
        device_id=xl_owner, device_id_type=MESH,
    )
    cot_ici.start()
    sent.append(cot_ici)
    cot_core = pltpu.make_async_remote_copy(
        src_ref=ct_ref, dst_ref=cot.at[z, c], send_sem=ss.at[sem_core], recv_sem=rs.at[sem_core],
        device_id=core_peer, device_id_type=MESH,
    )

    @pl.when(jnp.logical_not(same))
    def _():
        cot_core.start()

    q_core = copy(q_ref.at[:, other], qt.at[c], core_peer)

    def kv_direct(x):
        low, high = kvr.at[y * 4 + x * 2], kvr.at[y * 4 + x * 2 + 1]
        return (
            copy(low, low, y_right), copy(high, high, y_left),
            copy(high, high, y_right), copy(low, low, y_left),
        )

    def kv_forward(x):
        low, high = kvr.at[yl * 4 + x * 2], kvr.at[yr * 4 + x * 2 + 1]
        return copy(low, low, y_right), copy(high, high, y_left)

    def z_pair(right_slot, left_slot, h):
        a, b = cot.at[right_slot, h], cot.at[left_slot, h]
        return copy(a, a, z_right), copy(b, b, z_left)

    key_copy.wait()
    value_copy.wait()
    arrived(*core_first)
    kv_xh = copy(kvr.at[pl.ds(own, 2)], kvr.at[pl.ds(own, 2)], xh_peer)
    kv_mine = kv_direct(xh)
    w_right = copy(w_ref, wt.at[w_own], y_right)
    w_left = copy(w_ref, wt.at[w_own], y_left)

    @pl.when(same)
    def _():
        cot_copy.wait()
        cot_core.wait_recv()

    @pl.when(jnp.logical_not(same))
    def _():
        for h in range(2):
            pltpu.make_async_remote_copy(
                src_ref=ct_ref, dst_ref=cot.at[z, h], send_sem=ss.at[sem_ici],
                recv_sem=rs.at[sem_ici + h], device_id=xl_owner, device_id_type=MESH,
            ).wait_recv()

    z_one = [z_pair(z, z, h) for h in range(2)]
    w_xh = [copy(w_ref, wt.at[w_own], xh_peer)]

    acc[...] = jnp.zeros_like(acc)
    l_ref[...] = jnp.zeros_like(l_ref)
    m_ref[...] = jnp.full_like(m_ref, BLOCKED)
    pga[...] = jnp.zeros_like(pga)
    dq_t[...] = jnp.zeros_like(dq_t)
    query_copy.wait()
    weight_copy.wait()
    arrived(q_core)

    arrived(*kv_mine[:2])
    kv_mine_far = kv_forward(xh)
    arrived(kv_xh)
    kv_other = kv_direct(1 - xh)
    arrived(*z_one[0])
    z_two = [z_pair(zl, zr, 0)]

    ahead = (
        lax.broadcasted_iota(jnp.int32, (1, HALF, TOKENS), 2) % HALF
        - lax.broadcasted_iota(jnp.int32, (1, HALF, TOKENS), 1)
    )

    def residue_rows(slot, count):
        return kvr[pl.ds(slot, count), pl.ds(2 * TOKENS, 16), :].astype(F32)[:, 0:1, :]

    query_res = residue_rows(own, 2)
    query_res = jnp.concatenate([query_res[0:1], query_res[1:2]], axis=2)

    def tile_scores(yy, qi, ki):
        key_res = residue_rows(yy * 4, 4)
        key_res = jnp.concatenate([key_res, key_res], axis=2)
        bound = jnp.where(key_res <= query_res, 0, 1) - jnp.where(qi > ki, 4 * HALF, 0)
        rows = pl.multiple_of(ki * HALF, HALF)
        keys = kvr[pl.ds(yy * 4, 4), pl.ds(rows, HALF), :].reshape(4 * HALF, HEAD_DIM)
        values = kvr[pl.ds(yy * 4, 4), pl.ds(TOKENS + rows, HALF), :].reshape(4 * HALF, HEAD_DIM)
        query_rows = pl.ds(pl.multiple_of(qi * HALF, HALF), HALF)
        queries = qt[:, query_rows, :].reshape(TOKENS, HEAD_DIM)
        scores = mm_nt(keys, queries) * SCALE_LOG2
        seen = ahead >= bound
        scores = jnp.where(seen, scores.reshape(4, HALF, TOKENS), BLOCKED)
        return scores.reshape(4 * HALF, TOKENS), keys, values, queries

    def forward(yy):
        def tile(t, carry):
            qi, ki = (t + 1) // 2, t // 2
            scores, _, values, _ = tile_scores(yy, qi, ki)
            old = m_ref[qi]
            new = jnp.maximum(old, jnp.max(scores, axis=0, keepdims=True))
            probs = jnp.exp2(scores - new)
            shrink = jnp.exp2(old - new)
            m_ref[qi] = new
            l_ref[qi] = l_ref[qi] * shrink + jnp.sum(probs, axis=0, keepdims=True)
            acc[qi] = acc[qi] * shrink + mm_tn(values, probs.astype(BF16))
            return carry

        lax.fori_loop(0, 3, tile, 0)

    forward(y)
    arrived(w_right, w_left)
    w_low, w_high = wt.at[yl * 2 + xh, pl.ds(0, 160)], wt.at[yr * 2 + xh, pl.ds(160, 160)]
    w_far = (copy(w_low, w_low, y_right), copy(w_high, w_high, y_left))
    w_xh.append(copy(wt.at[yl * 2 + xh], wt.at[yl * 2 + xh], xh_peer))
    w_xh.append(copy(wt.at[yr * 2 + xh], wt.at[yr * 2 + xh], xh_peer))
    arrived(*z_one[1])
    z_two.append(z_pair(zl, zr, 1))
    arrived(*z_two[0])
    z_three = [z_pair((z + 6) % 8, (z + 2) % 8, 0)]
    arrived(*kv_other[:2])
    kv_other_far = kv_forward(1 - xh)
    arrived(*kv_mine[2:], *kv_other[2:])
    forward(yl)
    arrived(*w_far)
    w_xh.append(copy(wt.at[y2 * 2 + xh], wt.at[y2 * 2 + xh], xh_peer))
    arrived(*z_two[1])
    z_three.append(z_pair((z + 6) % 8, (z + 2) % 8, 1))
    forward(yr)
    arrived(*z_three[0])
    z_four = [copy(cot.at[(z + 5) % 8, 0], cot.at[(z + 5) % 8, 0], z_right)]
    arrived(*kv_mine_far, *kv_other_far)
    forward(y2)
    arrived(*z_three[1])
    z_four.append(copy(cot.at[(z + 3) % 8, 1], cot.at[(z + 3) % 8, 1], z_left))

    for qi in range(2):
        total = l_ref[qi]
        rows = (acc[qi] / total).astype(BF16)
        att_t[qi] = rows
        m_ref[qi] = m_ref[qi] + jnp.log2(total)
        wide = rows.astype(F32)
        for h in range(2):
            att[c, h, pl.ds(qi * HALF, HALF), :] = wide[:, h * HALF:(h + 1) * HALF].T.astype(BF16)
    att_core = copy(att.at[c], att.at[c], core_peer)
    arrived(*w_xh)
    arrived(att_core)
    for h in range(2):
        att_full[h] = jnp.concatenate([att[0, h], att[1, h]], axis=1)

    def w_block(i):
        return wt[(i % 4) * 2 + i // 4]

    def out_term(i, h):
        return mm_nt(w_block(i), att_full[h])

    def out_hop(step, long_chain, got):
        sends = []
        for side in range(2):
            h = side if long_chain else 1 - side
            target = (z + 4 - step) % 8 if side == 0 else (z + 4 + step) % 8
            term = out_term(target, h)
            if got is not None:
                arrived(got[side])
                term = term + out_in[side, step - 1, h].astype(F32)
            out_send[side, step, h] = term.astype(BF16)
            sends.append(
                copy(out_send.at[side, step, h], out_in.at[side, step, h], z_left if side else z_right)
            )
        return sends

    long_0 = out_hop(0, True, None)
    short_1 = out_hop(1, False, None)
    arrived(*z_four)

    def width_step(i, carry):
        weight = w_block(i)
        for h in range(2):
            term = mm_tn(weight, cot[i, h])
            pga[0, h] += term[:HEAD_DIM]
            pga[1, h] += term[HEAD_DIM:]
        return carry

    lax.fori_loop(0, 8, width_step, 0)
    pga_core = copy(pga.at[p], pga_in, core_peer)

    def gw_term(x, yy):
        i = x * 4 + yy
        return mm(cot[i, 0], att_full[0]) + mm(cot[i, 1], att_full[1])

    gw_over = []
    for i, yy in enumerate((y2, yr, yl, y)):
        gw_xsend[i] = gw_term(1 - xh, yy).astype(BF16)
        gw_over.append(copy(gw_xsend.at[i], gw_xin.at[i], xh_peer))
    long_1 = out_hop(1, True, long_0)

    arrived(pga_core)
    for h in range(2):
        rows = (pga[c, h] + pga_in[h]).astype(BF16)
        for qi in range(2):
            grad_t[qi, :, h * HALF:(h + 1) * HALF] = rows[:, qi * HALF:(qi + 1) * HALF]
    for qi in range(2):
        wide = grad_t[qi].astype(F32)
        delta[qi] = jnp.sum(wide * att_t[qi].astype(F32), axis=0, keepdims=True)
        grad[qi] = wide.T.astype(BF16)

    def backward(yy):
        df[...] = jnp.zeros_like(df)

        def tile(t, carry):
            qi, ki = (t + 1) // 2, t // 2
            scores, keys, values, queries = tile_scores(yy, qi, ki)
            probs = jnp.exp2(scores - m_ref[qi])
            grad_probs = mm(values, grad_t[qi])
            grad_scores = (probs * (grad_probs - delta[qi])).astype(BF16)
            rows = pl.ds(pl.multiple_of(ki * HALF, HALF), HALF)
            grad_keys = mm(grad_scores, queries).reshape(4, HALF, HEAD_DIM)
            grad_values = mm(probs.astype(BF16), grad[qi]).reshape(4, HALF, HEAD_DIM)
            df[:, 0, rows, :] += grad_keys
            df[:, 1, rows, :] += grad_values
            dq_t[qi] += mm_tn(keys, grad_scores)
            return carry

        lax.fori_loop(0, 3, tile, 0)

    near = pl.ds(2 * xh, 2)
    over = pl.ds(2 * (1 - xh), 2)

    backward(y2)
    d_send[0, 0] = df[near].astype(BF16)
    d_far_right = copy(d_send.at[0, 0], d_rin2, y_right)
    d_send[0, 1] = df[over].astype(BF16)
    d_far_left = copy(d_send.at[0, 1], d_lin2, y_left)
    short_2 = out_hop(2, False, short_1)

    arrived(gw_over[0])
    gw_send[0] = (gw_term(xh, y2) + gw_xin[0].astype(F32)).astype(BF16)
    gw_far = (
        copy(gw_send.at[0, pl.ds(0, 160)], gw_rin2, y_right),
        copy(gw_send.at[0, pl.ds(160, 160)], gw_lin2, y_left),
    )

    backward(yr)
    d_send[1, 1] = df[over].astype(BF16)
    d_right = [copy(d_send.at[1, 1], d_rin.at[1], y_right)]
    long_2 = out_hop(2, True, long_1)
    arrived(d_far_right)
    d_send[1, 0] = (df[near] + d_rin2[...].astype(F32)).astype(BF16)
    d_right.append(copy(d_send.at[1, 0], d_rin.at[0], y_right))

    backward(yl)
    arrived(d_far_left)
    d_send[2, 1] = (df[over] + d_lin2[...].astype(F32)).astype(BF16)
    d_left = [copy(d_send.at[2, 1], d_lin.at[1], y_left)]
    d_send[2, 0] = df[near].astype(BF16)
    d_left.append(copy(d_send.at[2, 0], d_lin.at[0], y_left))
    short_3 = out_hop(3, False, short_2)

    arrived(*gw_far)
    arrived(*gw_over[1:])
    low, high = pl.ds(0, 160), pl.ds(160, 160)
    term = gw_term(xh, yr) + gw_xin[1].astype(F32)
    gw_send[1, low] = (term[:160] + gw_rin2[...].astype(F32)).astype(BF16)
    gw_send[1, high] = term[160:].astype(BF16)
    term = gw_term(xh, yl) + gw_xin[2].astype(F32)
    gw_send[2, low] = term[:160].astype(BF16)
    gw_send[2, high] = (term[160:] + gw_lin2[...].astype(F32)).astype(BF16)
    gw_near = (copy(gw_send.at[1], gw_rin, y_right), copy(gw_send.at[2], gw_lin, y_left))

    backward(y)
    long_3 = out_hop(3, True, long_2)
    for qi in range(2):
        for h in range(2):
            dq_b[h, pl.ds(qi * HALF, HALF), :] = dq_t[qi, :, h * HALF:(h + 1) * HALF].T * SCALE
    dq_core = copy(dq_b.at[p], dq_in, core_peer)

    arrived(d_right[0], d_left[0])
    d_send[3, 1] = (df[over] + d_rin[1].astype(F32) + d_lin[1].astype(F32)).astype(BF16)
    d_over = copy(d_send.at[3, 1], d_x, xh_peer)

    first = c == 0

    def place(ref, mine, theirs):
        ref[:, :HEAD_DIM] = jnp.where(first, mine, theirs)
        ref[:, HEAD_DIM:] = jnp.where(first, theirs, mine)

    arrived(dq_core)
    place(dq_ref, dq_b[c], dq_in[...])
    store(1, dq_ref, dq_hbm)

    arrived(*short_3)
    for h in range(2):
        out_fin[h] = out_term(z, h) + out_in[1 - h, 3, h].astype(F32)
    arrived(*long_3)
    for h in range(2):
        out_send[0, 4, h] = (out_fin[h] + out_in[h, 3, h].astype(F32)).astype(BF16)
    pair_ici, pair_core = take(2), take()
    to_peers = [
        pltpu.make_async_remote_copy(
            src_ref=out_send.at[0, 4, h], dst_ref=out_pair_ici, send_sem=ss.at[pair_ici + h],
            recv_sem=rs.at[pair_ici], device_id=xl_peers[h], device_id_type=MESH,
        )
        for h in range(2)
    ]
    to_core = pltpu.make_async_remote_copy(
        src_ref=out_send.at[0, 4, p], dst_ref=out_pair_core, send_sem=ss.at[pair_core],
        recv_sem=rs.at[pair_core], device_id=core_peer, device_id_type=MESH,
    )

    @pl.when(same)
    def _():
        to_core.start()

    @pl.when(jnp.logical_not(same))
    def _():
        to_peers[0].start()
        to_peers[1].start()

    arrived(d_right[1], d_left[1])
    arrived(d_over)
    for part in range(2):
        total = (
            df[near, part]
            + d_rin[0, :, part].astype(F32)
            + d_lin[0, :, part].astype(F32)
            + d_x[:, part].astype(F32)
        )
        fin[:, part] = total * SCALE if part == 0 else total
    fin_core = copy(fin.at[p], fin_in, core_peer)

    arrived(*gw_near)
    gw_ref[...] = (
        gw_term(xh, y) + gw_xin[3].astype(F32) + gw_rin[...].astype(F32) + gw_lin[...].astype(F32)
    )
    store(4, gw_ref, gw_hbm)

    arrived(fin_core)
    place(dk_ref, fin[c, 0], fin_in[0])
    store(2, dk_ref, dk_hbm)
    place(dv_ref, fin[c, 1], fin_in[1])
    store(3, dv_ref, dv_hbm)

    arrived(to_peers[0])

    @pl.when(same)
    def _():
        out_ref[...] = out_send[0, 4, c].astype(F32) + out_pair_ici[...].astype(F32)
        to_core.wait_send()

    @pl.when(jnp.logical_not(same))
    def _():
        to_core.wait_recv()
        out_ref[...] = out_pair_core[...].astype(F32) + out_pair_ici[...].astype(F32)
        to_peers[0].wait_send()
        to_peers[1].wait_send()
        cot_core.wait_send()

    store(0, out_ref, out_hbm)
    for d in sent:
        d.wait_send()
    for d in stores:
        d.wait()
    assert used[0] <= SEMS, used[0]


def fused(pos, q, k, v, w, ct):
    vm = pltpu.VMEM
    scratch = [
        vm((16, 2 * TOKENS + 16, HEAD_DIM), BF16),
        vm((16, HEAD_DIM), BF16),
        vm((2, TOKENS, HEAD_DIM), BF16),
        vm((8, COLS, FEATS), BF16),
        vm((8, 2, COLS, TOKENS), BF16),
        vm((2, 1, TOKENS), F32),
        vm((2, 1, TOKENS), F32),
        vm((2, HEAD_DIM, TOKENS), F32),
        vm((2, HEAD_DIM, TOKENS), BF16),
        vm((2, 2, TOKENS, HEAD_DIM), BF16),
        vm((2, TOKENS, FEATS), BF16),
        vm((2, 2, HEAD_DIM, TOKENS), F32),
        vm((2, HEAD_DIM, TOKENS), F32),
        vm((2, HEAD_DIM, TOKENS), BF16),
        vm((2, TOKENS, HEAD_DIM), BF16),
        vm((2, 1, TOKENS), F32),
        vm((2, 5, 2, COLS, TOKENS), BF16),
        vm((2, 4, 2, COLS, TOKENS), BF16),
        vm((2, COLS, TOKENS), F32),
        vm((COLS, TOKENS), BF16),
        vm((COLS, TOKENS), BF16),
        vm((4, COLS, FEATS), BF16),
        vm((4, COLS, FEATS), BF16),
        vm((3, COLS, FEATS), BF16),
        vm((COLS // 2, FEATS), BF16),
        vm((COLS // 2, FEATS), BF16),
        vm((COLS, FEATS), BF16),
        vm((COLS, FEATS), BF16),
        vm((4, 2, TOKENS, HEAD_DIM), F32),
        vm((4, 2, 2, 2, TOKENS, HEAD_DIM), BF16),
        vm((2, 2, TOKENS, HEAD_DIM), BF16),
        vm((2, 2, TOKENS, HEAD_DIM), BF16),
        vm((2, 2, 2, TOKENS, HEAD_DIM), BF16),
        vm((2, 2, 2, TOKENS, HEAD_DIM), BF16),
        vm((2, 2, TOKENS, HEAD_DIM), BF16),
        vm((2, 2, TOKENS, HEAD_DIM), F32),
        vm((2, TOKENS, HEAD_DIM), F32),
        vm((2, HEAD_DIM, TOKENS), F32),
        vm((2, TOKENS, HEAD_DIM), F32),
        vm((TOKENS, HEAD_DIM), F32),
        pltpu.SemaphoreType.DMA((SEMS,)),
        pltpu.SemaphoreType.DMA((SEMS,)),
        pltpu.SemaphoreType.DMA((10,)),
    ]
    in_hbm = pl.BlockSpec(memory_space=pl.ANY)
    return pl.pallas_call(
        kernel,
        name="attention_core",
        out_shape=OUT_SHAPES,
        in_specs=[pl.BlockSpec(memory_space=pltpu.SMEM)] + [in_hbm] * 5,
        out_specs=(in_hbm,) * 5,
        scratch_shapes=[vm(d.shape, d.dtype) for d in OUT_SHAPES] + scratch,
        compiler_params=pltpu.CompilerParams(
            collective_id=0, has_side_effects=True, vmem_limit_bytes=62 << 20
        ),
    )(pos, q, k, v, w, ct)


OUT_SHAPES = (
    jax.ShapeDtypeStruct((COLS, TOKENS), F32),
    jax.ShapeDtypeStruct((TOKENS, FEATS), F32),
    jax.ShapeDtypeStruct((TOKENS, FEATS), F32),
    jax.ShapeDtypeStruct((TOKENS, FEATS), F32),
    jax.ShapeDtypeStruct((COLS, FEATS), F32),
)


def store_kernel(*refs):
    results, outs, held, sems = refs[:5], refs[5:10], refs[10:15], refs[15]
    loads = [pltpu.make_async_copy(results[i], held[i], sems.at[0, i]) for i in range(5)]
    stores = [pltpu.make_async_copy(held[i], outs[i], sems.at[1, i]) for i in range(5)]
    for d in loads:
        d.start()
    for load, store in zip(loads, stores):
        load.wait()
        store.start()
    for d in stores:
        d.wait()


def stored(*results):
    return pl.pallas_call(
        store_kernel,
        name="store_results",
        out_shape=OUT_SHAPES,
        in_specs=[pl.BlockSpec(memory_space=pl.ANY)] * 5,
        out_specs=(pl.BlockSpec(memory_space=pl.ANY),) * 5,
        scratch_shapes=[pltpu.VMEM(d.shape, d.dtype) for d in OUT_SHAPES]
        + [pltpu.SemaphoreType.DMA((2, 5))],
        compiler_params=pltpu.CompilerParams(vmem_limit_bytes=62 << 20),
    )(*results)


def shards(query_states, key_states, value_states, positions, out_weight, cotangent):
    results = fused(
        positions, query_states, key_states, value_states, out_weight.T, cotangent.T
    )
    out_t, grad_queries, grad_keys, grad_values, gw_t = stored(*results)
    return out_t.T, grad_queries, grad_keys, grad_values, gw_t.T


def solution(mesh):
    in_specs = (
        P("seq", "fsdp"),
        P("seq", "fsdp"),
        P("seq", "fsdp"),
        P("seq"),
        P("fsdp", "seq"),
        P("seq", "fsdp"),
    )
    out_specs = (
        P("seq", "fsdp"),
        P("seq", "fsdp"),
        P("seq", "fsdp"),
        P("seq", "fsdp"),
        P("fsdp", "seq"),
    )
    return jax.shard_map(shards, mesh=mesh, in_specs=in_specs, out_specs=out_specs, check_vma=False)
```

time: 103 us -> 86.3 us (0.84)
  local copies, waits for them, and re-layouts: 9.28 us -> 0 us
  Pallas kernels: 90.8 us -> 85.5 us
  between operations: 2.63 us -> 0.64 us
    unnamed x17 -> x0, local copies, waits for them, and re-layouts: 8.77 us -> none
    pallas_call x1 -> x2, Pallas kernels: 90.8 us -> 85.5 us  [the longest x1 83.4 us: fused(): pl.pallas_call(kernel, name='attention_core', out_shape=OUT_SHAPES, in_sp...]
where the time goes in v2:
time: 86.3 us; the launch traced here: 86.2 us
  Pallas kernels  85.5 us (99%)
    pallas_call x1, Pallas kernels, fused(): pl.pallas_call(kernel, name='attention_core', out_shape=OUT_SHAPES, in_sp...  83.4 us
    pallas_call x1, Pallas kernels, stored(): pl.pallas_call(store_kernel, name='store_results', out_shape=OUT_SHAPES,...  2.15 us

profile of v2, /device:TPU:1, one launch (start us, length us, event | category | flops | bytes accessed | tf_op | source)
XLA Modules:
  0.0 86.2 jit_solution(7377992260891883997)
XLA Ops:
  0.6 83.4 %attention_core.1 = (f32[320,256]{1,0:T(8,128)}, f32[256,256]{1,0:T(8,128)}, f32[256,256]{1,0:T(8,128)}, f32[256,256]{1,0:T(8,128)}, f32[320,256]{1,0:T(8,128)}) custom-call(s32[256]{0:T(256)} %pos_ref.1, bf16[256,256]{1,0:T(8,128)(2,1)} %q_ref.1, bf16[256,256]{1,0:T(8,128)(2,1)} %k_ref.1, bf16[256,256]{1,0:T(8,128)(2,1)} %v_ref.1, ...), custom_call_target="tpu_custom_call" | custom-call | tf_op jit(solution)/shard_map/attention_core/pallas_call | solution.py:548
  84.0 2.2 %store_results.1 = (f32[320,256]{1,0:T(8,128)}, f32[256,256]{1,0:T(8,128)}, f32[256,256]{1,0:T(8,128)}, f32[256,256]{1,0:T(8,128)}, f32[320,256]{1,0:T(8,128)}) custom-call(f32[320,256]{1,0:T(8,128)} %get-tuple-element.15.refs_0_, f32[256,256]{1,0:T(8,128)} %get-tuple-element.16.refs_1_, f32[256,256]{1,0:T(8,128)} %get-tuple-element.17.refs_2_, ...), custom_call_target="tpu_custom_call" | custom-call | tf_op jit(solution)/shard_map/store_results/pallas_call | solution.py:584

commit v3 on v2

--- a/solution.py
+++ b/solution.py
@@ -18,7 +18,7 @@
 SCALE = HEAD_DIM ** (-0.5)
 SCALE_LOG2 = SCALE * math.log2(math.e)
 BLOCKED = -1e30
-SEMS = 100
+SEMS = 112
 
 
 def mm(a, b):
@@ -42,7 +42,7 @@
     pga, pga_in, grad_t, grad, delta,
     out_send, out_in, out_fin, out_pair_ici, out_pair_core,
     gw_xsend, gw_xin, gw_send, gw_rin2, gw_lin2, gw_rin, gw_lin,
-    df, d_send, d_rin2, d_lin2, d_rin, d_lin, d_x, fin, fin_in,
+    df, df_right, d_send, d_rin2, d_lin2, d_rin, d_lin, d_x, fin, fin_in,
     dq_t, dq_b, dq_in,
     ss, rs, ls,
 ):
@@ -115,13 +115,40 @@
     weight_copy.start()
 
     barrier = pltpu.get_barrier_semaphore()
-    peers = [core_peer, xh_peer, y_right, y_left, z_right, z_left] + xl_peers
+    z_cross = [dev(xh, y, p, zr, xl), dev(xh, y, p, zl, xl)]
+    peers = [core_peer, xh_peer, y_right, y_left, z_right, z_left] + xl_peers + z_cross
     for peer in peers:
         pl.semaphore_signal(barrier, inc=1, device_id=peer, device_id_type=MESH)
     residue = jnp.full((16, HEAD_DIM), (pos_ref[0] % 16).astype(F32)).astype(BF16)
     res[...] = residue
     kvr[own + c, res_rows, :] = residue
+    key_copy.wait()
+    value_copy.wait()
     pl.semaphore_wait(barrier, len(peers))
+
+    sem_ici, sem_core, sem_z = take(2), take(), take(4)
+    z_owner = [dev(xh, y, xl, zr, xl), dev(xh, y, xl, zl, xl)]
+
+    def cot_copy_to(h, src, to, send, recv):
+        return pltpu.make_async_remote_copy(
+            src_ref=src, dst_ref=cot.at[z, h], send_sem=ss.at[send], recv_sem=rs.at[recv],
+            device_id=to, device_id_type=MESH,
+        )
+
+    cot_ici = cot_copy_to(c, ct_ref, xl_owner, sem_ici, sem_ici + c)
+    cot_core = cot_copy_to(c, ct_ref, core_peer, sem_core, sem_core)
+    cot_z = [
+        cot_copy_to(c, ct_ref, z_owner[side], sem_z + side, sem_z + 2 * side + c) for side in range(2)
+    ]
+    sem_own = take(4)
+    cot_own = [
+        [
+            cot_copy_to(h, cot.at[z, h], to, sem_own + 2 * side + h, sem_z + 2 * side + h)
+            for side, to in enumerate((z_right, z_left))
+        ]
+        for h in range(2)
+    ]
+    cot_ici.start()
 
     core_first = (
         copy(k_ref.at[:, other], kvr.at[own + c, key_rows], core_peer),
@@ -129,46 +156,28 @@
         copy(res, kvr.at[own + c, res_rows], core_peer),
     )
 
-    sem_ici, sem_core = take(2), take()
-    cot_ici = pltpu.make_async_remote_copy(
-        src_ref=ct_ref, dst_ref=cot.at[z, c], send_sem=ss.at[sem_ici], recv_sem=rs.at[sem_ici + c],
-        device_id=xl_owner, device_id_type=MESH,
-    )
-    cot_ici.start()
-    sent.append(cot_ici)
-    cot_core = pltpu.make_async_remote_copy(
-        src_ref=ct_ref, dst_ref=cot.at[z, c], send_sem=ss.at[sem_core], recv_sem=rs.at[sem_core],
-        device_id=core_peer, device_id_type=MESH,
-    )
+    def kv_send(slot, *targets):
+        block = kvr.at[slot]
+        return [copy(block, block, to) for to in targets]
+
+    kv_c = kv_send(own + c, y_right, y_left, xh_peer)
+    for d in cot_z:
+        d.start()
 
     @pl.when(jnp.logical_not(same))
     def _():
         cot_core.start()
 
+    w_right = copy(w_ref, wt.at[w_own], y_right)
+    w_left = copy(w_ref, wt.at[w_own], y_left)
     q_core = copy(q_ref.at[:, other], qt.at[c], core_peer)
-
-    def kv_direct(x):
-        low, high = kvr.at[y * 4 + x * 2], kvr.at[y * 4 + x * 2 + 1]
-        return (
-            copy(low, low, y_right), copy(high, high, y_left),
-            copy(high, high, y_right), copy(low, low, y_left),
-        )
-
-    def kv_forward(x):
-        low, high = kvr.at[yl * 4 + x * 2], kvr.at[yr * 4 + x * 2 + 1]
-        return copy(low, low, y_right), copy(high, high, y_left)
 
     def z_pair(right_slot, left_slot, h):
         a, b = cot.at[right_slot, h], cot.at[left_slot, h]
         return copy(a, a, z_right), copy(b, b, z_left)
 
-    key_copy.wait()
-    value_copy.wait()
     arrived(*core_first)
-    kv_xh = copy(kvr.at[pl.ds(own, 2)], kvr.at[pl.ds(own, 2)], xh_peer)
-    kv_mine = kv_direct(xh)
-    w_right = copy(w_ref, wt.at[w_own], y_right)
-    w_left = copy(w_ref, wt.at[w_own], y_left)
+    kv_p = kv_send(own + p, y_right, y_left, xh_peer)
 
     @pl.when(same)
     def _():
@@ -178,12 +187,10 @@
     @pl.when(jnp.logical_not(same))
     def _():
         for h in range(2):
-            pltpu.make_async_remote_copy(
-                src_ref=ct_ref, dst_ref=cot.at[z, h], send_sem=ss.at[sem_ici],
-                recv_sem=rs.at[sem_ici + h], device_id=xl_owner, device_id_type=MESH,
-            ).wait_recv()
-
-    z_one = [z_pair(z, z, h) for h in range(2)]
+            cot_copy_to(h, ct_ref, xl_owner, sem_ici, sem_ici + h).wait_recv()
+            for d in cot_own[h]:
+                d.start()
+
     w_xh = [copy(w_ref, wt.at[w_own], xh_peer)]
 
     acc[...] = jnp.zeros_like(acc)
@@ -195,12 +202,26 @@
     weight_copy.wait()
     arrived(q_core)
 
-    arrived(*kv_mine[:2])
-    kv_mine_far = kv_forward(xh)
-    arrived(kv_xh)
-    kv_other = kv_direct(1 - xh)
-    arrived(*z_one[0])
-    z_two = [z_pair(zl, zr, 0)]
+    kv_far = []
+    over_own = y * 4 + (1 - xh) * 2
+
+    arrived(kv_c[0])
+    kv_far += kv_send(yl * 4 + xh * 2 + c, y_right)
+    arrived(kv_c[1], kv_c[2])
+    kv_over_c = kv_send(over_own + c, y_right, y_left)
+    z_two = []
+    for h in range(2):
+        for d in cot_own[h]:
+            d.wait_recv()
+        z_two.append(z_pair(zl, zr, h))
+    arrived(w_right, w_left)
+    w_low, w_high = wt.at[yl * 2 + xh, pl.ds(0, 160)], wt.at[yr * 2 + xh, pl.ds(160, 160)]
+    w_far = (copy(w_low, w_low, y_right), copy(w_high, w_high, y_left))
+    w_xh.append(copy(wt.at[yl * 2 + xh], wt.at[yl * 2 + xh], xh_peer))
+    w_xh.append(copy(wt.at[yr * 2 + xh], wt.at[yr * 2 + xh], xh_peer))
+    arrived(*kv_p)
+    kv_over_p = kv_send(over_own + p, y_right, y_left)
+    kv_far += kv_send(yr * 4 + xh * 2 + p, y_left)
 
     ahead = (
         lax.broadcasted_iota(jnp.int32, (1, HALF, TOKENS), 2) % HALF
@@ -243,30 +264,24 @@
         lax.fori_loop(0, 3, tile, 0)
 
     forward(y)
-    arrived(w_right, w_left)
-    w_low, w_high = wt.at[yl * 2 + xh, pl.ds(0, 160)], wt.at[yr * 2 + xh, pl.ds(160, 160)]
-    w_far = (copy(w_low, w_low, y_right), copy(w_high, w_high, y_left))
-    w_xh.append(copy(wt.at[yl * 2 + xh], wt.at[yl * 2 + xh], xh_peer))
-    w_xh.append(copy(wt.at[yr * 2 + xh], wt.at[yr * 2 + xh], xh_peer))
-    arrived(*z_one[1])
-    z_two.append(z_pair(zl, zr, 1))
     arrived(*z_two[0])
     z_three = [z_pair((z + 6) % 8, (z + 2) % 8, 0)]
-    arrived(*kv_other[:2])
-    kv_other_far = kv_forward(1 - xh)
-    arrived(*kv_mine[2:], *kv_other[2:])
-    forward(yl)
+    arrived(*kv_over_c)
+    kv_far += kv_send(yl * 4 + (1 - xh) * 2 + c, y_right)
+    arrived(*z_two[1])
+    z_three.append(z_pair((z + 6) % 8, (z + 2) % 8, 1))
     arrived(*w_far)
     w_xh.append(copy(wt.at[y2 * 2 + xh], wt.at[y2 * 2 + xh], xh_peer))
-    arrived(*z_two[1])
-    z_three.append(z_pair((z + 6) % 8, (z + 2) % 8, 1))
-    forward(yr)
+    arrived(*kv_over_p)
+    kv_far += kv_send(yr * 4 + (1 - xh) * 2 + p, y_left)
+    forward(yl)
     arrived(*z_three[0])
     z_four = [copy(cot.at[(z + 5) % 8, 0], cot.at[(z + 5) % 8, 0], z_right)]
-    arrived(*kv_mine_far, *kv_other_far)
-    forward(y2)
+    forward(yr)
     arrived(*z_three[1])
     z_four.append(copy(cot.at[(z + 3) % 8, 1], cot.at[(z + 3) % 8, 1], z_left))
+    arrived(*kv_far)
+    forward(y2)
 
     for qi in range(2):
         total = l_ref[qi]
@@ -278,12 +293,23 @@
             att[c, h, pl.ds(qi * HALF, HALF), :] = wide[:, h * HALF:(h + 1) * HALF].T.astype(BF16)
     att_core = copy(att.at[c], att.at[c], core_peer)
     arrived(*w_xh)
+
+    def w_block(i):
+        return wt[(i % 4) * 2 + i // 4]
+
+    def width_step(k, carry):
+        i = (z + 5 + k) % 8
+        weight = w_block(i)
+        for h in range(2):
+            term = mm_tn(weight, cot[i, h])
+            pga[0, h] += term[:HEAD_DIM]
+            pga[1, h] += term[HEAD_DIM:]
+        return carry
+
+    lax.fori_loop(0, 7, width_step, 0)
     arrived(att_core)
     for h in range(2):
         att_full[h] = jnp.concatenate([att[0, h], att[1, h]], axis=1)
-
-    def w_block(i):
-        return wt[(i % 4) * 2 + i // 4]
 
     def out_term(i, h):
         return mm_nt(w_block(i), att_full[h])
@@ -307,15 +333,7 @@
     short_1 = out_hop(1, False, None)
     arrived(*z_four)
 
-    def width_step(i, carry):
-        weight = w_block(i)
-        for h in range(2):
-            term = mm_tn(weight, cot[i, h])
-            pga[0, h] += term[:HEAD_DIM]
-            pga[1, h] += term[HEAD_DIM:]
-        return carry
-
-    lax.fori_loop(0, 8, width_step, 0)
+    width_step(7, 0)
     pga_core = copy(pga.at[p], pga_in, core_peer)
 
     def gw_term(x, yy):
@@ -326,7 +344,6 @@
     for i, yy in enumerate((y2, yr, yl, y)):
         gw_xsend[i] = gw_term(1 - xh, yy).astype(BF16)
         gw_over.append(copy(gw_xsend.at[i], gw_xin.at[i], xh_peer))
-    long_1 = out_hop(1, True, long_0)
 
     arrived(pga_core)
     for h in range(2):
@@ -338,7 +355,7 @@
         delta[qi] = jnp.sum(wide * att_t[qi].astype(F32), axis=0, keepdims=True)
         grad[qi] = wide.T.astype(BF16)
 
-    def backward(yy):
+    def backward(yy, df):
         df[...] = jnp.zeros_like(df)
 
         def tile(t, carry):
@@ -360,12 +377,12 @@
     near = pl.ds(2 * xh, 2)
     over = pl.ds(2 * (1 - xh), 2)
 
-    backward(y2)
+    backward(y2, df)
     d_send[0, 0] = df[near].astype(BF16)
     d_far_right = copy(d_send.at[0, 0], d_rin2, y_right)
     d_send[0, 1] = df[over].astype(BF16)
     d_far_left = copy(d_send.at[0, 1], d_lin2, y_left)
-    short_2 = out_hop(2, False, short_1)
+    long_1 = out_hop(1, True, long_0)
 
     arrived(gw_over[0])
     gw_send[0] = (gw_term(xh, y2) + gw_xin[0].astype(F32)).astype(BF16)
@@ -374,21 +391,20 @@
         copy(gw_send.at[0, pl.ds(160, 160)], gw_lin2, y_left),
     )
 
-    backward(yr)
-    d_send[1, 1] = df[over].astype(BF16)
+    backward(yr, df_right)
+    d_send[1, 1] = df_right[over].astype(BF16)
     d_right = [copy(d_send.at[1, 1], d_rin.at[1], y_right)]
-    long_2 = out_hop(2, True, long_1)
-    arrived(d_far_right)
-    d_send[1, 0] = (df[near] + d_rin2[...].astype(F32)).astype(BF16)
-    d_right.append(copy(d_send.at[1, 0], d_rin.at[0], y_right))
-
-    backward(yl)
+    short_2 = out_hop(2, False, short_1)
+    backward(yl, df)
     arrived(d_far_left)
     d_send[2, 1] = (df[over] + d_lin2[...].astype(F32)).astype(BF16)
     d_left = [copy(d_send.at[2, 1], d_lin.at[1], y_left)]
+    arrived(d_far_right)
+    d_send[1, 0] = (df_right[near] + d_rin2[...].astype(F32)).astype(BF16)
+    d_right.append(copy(d_send.at[1, 0], d_rin.at[0], y_right))
     d_send[2, 0] = df[near].astype(BF16)
     d_left.append(copy(d_send.at[2, 0], d_lin.at[0], y_left))
-    short_3 = out_hop(3, False, short_2)
+    long_2 = out_hop(2, True, long_1)
 
     arrived(*gw_far)
     arrived(*gw_over[1:])
@@ -401,12 +417,13 @@
     gw_send[2, high] = (term[160:] + gw_lin2[...].astype(F32)).astype(BF16)
     gw_near = (copy(gw_send.at[1], gw_rin, y_right), copy(gw_send.at[2], gw_lin, y_left))
 
-    backward(y)
-    long_3 = out_hop(3, True, long_2)
+    backward(y, df)
+    short_3 = out_hop(3, False, short_2)
     for qi in range(2):
         for h in range(2):
             dq_b[h, pl.ds(qi * HALF, HALF), :] = dq_t[qi, :, h * HALF:(h + 1) * HALF].T * SCALE
     dq_core = copy(dq_b.at[p], dq_in, core_peer)
+    long_3 = out_hop(3, True, long_2)
 
     arrived(d_right[0], d_left[0])
     d_send[3, 1] = (df[over] + d_rin[1].astype(F32) + d_lin[1].astype(F32)).astype(BF16)
@@ -488,6 +505,13 @@
         to_peers[0].wait_send()
         to_peers[1].wait_send()
         cot_core.wait_send()
+        for pair in cot_own:
+            for d in pair:
+                d.wait_send()
+
+    cot_ici.wait_send()
+    for d in cot_z:
+        d.wait_send()
 
     store(0, out_ref, out_hbm)
     for d in sent:
@@ -529,6 +553,7 @@
         vm((COLS, FEATS), BF16),
         vm((COLS, FEATS), BF16),
         vm((4, 2, TOKENS, HEAD_DIM), F32),
+        vm((4, 2, TOKENS, HEAD_DIM), F32),
         vm((4, 2, 2, 2, TOKENS, HEAD_DIM), BF16),
         vm((2, 2, TOKENS, HEAD_DIM), BF16),
         vm((2, 2, TOKENS, HEAD_DIM), BF16),

time: 86.3 us -> 81.5 us (0.944)
  Pallas kernels: 85.5 us -> 80.7 us
    pallas_call x1, Pallas kernels: 83.4 us -> 78.6 us  [fused(): pl.pallas_call(kernel, name='attention_core', out_shape=OUT_SHAPES, in_sp...]
where the time goes in v3:
time: 81.5 us; the launch traced here: 81.4 us
  Pallas kernels  80.7 us (99%)
    pallas_call x1, Pallas kernels, fused(): pl.pallas_call(kernel, name='attention_core', out_shape=OUT_SHAPES, in_sp...  78.6 us
    pallas_call x1, Pallas kernels, stored(): pl.pallas_call(store_kernel, name='store_results', out_shape=OUT_SHAPES,...  2.15 us

profile of v3, /device:TPU:1, one launch (start us, length us, event | category | flops | bytes accessed | tf_op | source)
XLA Modules:
  0.0 81.4 jit_solution(1661250280946079602)
XLA Ops:
  0.6 78.6 %attention_core.1 = (f32[320,256]{1,0:T(8,128)}, f32[256,256]{1,0:T(8,128)}, f32[256,256]{1,0:T(8,128)}, f32[256,256]{1,0:T(8,128)}, f32[320,256]{1,0:T(8,128)}) custom-call(s32[256]{0:T(256)} %pos_ref.1, bf16[256,256]{1,0:T(8,128)(2,1)} %q_ref.1, bf16[256,256]{1,0:T(8,128)(2,1)} %k_ref.1, bf16[256,256]{1,0:T(8,128)(2,1)} %v_ref.1, ...), custom_call_target="tpu_custom_call" | custom-call | tf_op jit(solution)/shard_map/attention_core/pallas_call | solution.py:573
  79.2 2.2 %store_results.1 = (f32[320,256]{1,0:T(8,128)}, f32[256,256]{1,0:T(8,128)}, f32[256,256]{1,0:T(8,128)}, f32[256,256]{1,0:T(8,128)}, f32[320,256]{1,0:T(8,128)}) custom-call(f32[320,256]{1,0:T(8,128)} %get-tuple-element.15.refs_0_, f32[256,256]{1,0:T(8,128)} %get-tuple-element.16.refs_1_, f32[256,256]{1,0:T(8,128)} %get-tuple-element.17.refs_2_, ...), custom_call_target="tpu_custom_call" | custom-call | tf_op jit(solution)/shard_map/store_results/pallas_call | solution.py:609

commit v4 on v3

--- a/solution.py
+++ b/solution.py
@@ -116,7 +116,8 @@
 
     barrier = pltpu.get_barrier_semaphore()
     z_cross = [dev(xh, y, p, zr, xl), dev(xh, y, p, zl, xl)]
-    peers = [core_peer, xh_peer, y_right, y_left, z_right, z_left] + xl_peers + z_cross
+    xh_cross = dev(1 - xh, y, p, z, xl)
+    peers = [core_peer, xh_peer, y_right, y_left, z_right, z_left] + xl_peers + z_cross + [xh_cross]
     for peer in peers:
         pl.semaphore_signal(barrier, inc=1, device_id=peer, device_id_type=MESH)
     residue = jnp.full((16, HEAD_DIM), (pos_ref[0] % 16).astype(F32)).astype(BF16)
@@ -127,7 +128,8 @@
     pl.semaphore_wait(barrier, len(peers))
 
     sem_ici, sem_core, sem_z = take(2), take(), take(4)
-    z_owner = [dev(xh, y, xl, zr, xl), dev(xh, y, xl, zl, xl)]
+    z_lead = dev(xh, y, xl, jnp.where(c == 0, zr, zl), xl)
+    z_trail = dev(xh, y, xl, jnp.where(c == 0, zl, zr), xl)
 
     def cot_copy_to(h, src, to, send, recv):
         return pltpu.make_async_remote_copy(
@@ -137,9 +139,8 @@
 
     cot_ici = cot_copy_to(c, ct_ref, xl_owner, sem_ici, sem_ici + c)
     cot_core = cot_copy_to(c, ct_ref, core_peer, sem_core, sem_core)
-    cot_z = [
-        cot_copy_to(c, ct_ref, z_owner[side], sem_z + side, sem_z + 2 * side + c) for side in range(2)
-    ]
+    cot_lead = cot_copy_to(c, ct_ref, z_lead, sem_z, sem_z + 3 * c)
+    cot_trail = cot_copy_to(c, ct_ref, z_trail, sem_z + 1, sem_z + 2 - c)
     sem_own = take(4)
     cot_own = [
         [
@@ -161,8 +162,7 @@
         return [copy(block, block, to) for to in targets]
 
     kv_c = kv_send(own + c, y_right, y_left, xh_peer)
-    for d in cot_z:
-        d.start()
+    cot_lead.start()
 
     @pl.when(jnp.logical_not(same))
     def _():
@@ -172,12 +172,14 @@
     w_left = copy(w_ref, wt.at[w_own], y_left)
     q_core = copy(q_ref.at[:, other], qt.at[c], core_peer)
 
-    def z_pair(right_slot, left_slot, h):
-        a, b = cot.at[right_slot, h], cot.at[left_slot, h]
+    def z_pair(right_slot, left_slot, lead):
+        a = cot.at[right_slot % 8, 0 if lead else 1]
+        b = cot.at[left_slot % 8, 1 if lead else 0]
         return copy(a, a, z_right), copy(b, b, z_left)
 
     arrived(*core_first)
     kv_p = kv_send(own + p, y_right, y_left, xh_peer)
+    cot_trail.start()
 
     @pl.when(same)
     def _():
@@ -188,8 +190,8 @@
     def _():
         for h in range(2):
             cot_copy_to(h, ct_ref, xl_owner, sem_ici, sem_ici + h).wait_recv()
-            for d in cot_own[h]:
-                d.start()
+        cot_own[0][0].start()
+        cot_own[1][1].start()
 
     w_xh = [copy(w_ref, wt.at[w_own], xh_peer)]
 
@@ -209,16 +211,21 @@
     kv_far += kv_send(yl * 4 + xh * 2 + c, y_right)
     arrived(kv_c[1], kv_c[2])
     kv_over_c = kv_send(over_own + c, y_right, y_left)
-    z_two = []
-    for h in range(2):
-        for d in cot_own[h]:
-            d.wait_recv()
-        z_two.append(z_pair(zl, zr, h))
+
+    @pl.when(jnp.logical_not(same))
+    def _():
+        cot_own[1][0].start()
+        cot_own[0][1].start()
+
+    arrived(cot_own[0][0], cot_own[1][1])
+    z_lead_two = z_pair(z + 7, z + 1, True)
     arrived(w_right, w_left)
     w_low, w_high = wt.at[yl * 2 + xh, pl.ds(0, 160)], wt.at[yr * 2 + xh, pl.ds(160, 160)]
     w_far = (copy(w_low, w_low, y_right), copy(w_high, w_high, y_left))
     w_xh.append(copy(wt.at[yl * 2 + xh], wt.at[yl * 2 + xh], xh_peer))
     w_xh.append(copy(wt.at[yr * 2 + xh], wt.at[yr * 2 + xh], xh_peer))
+    arrived(cot_own[1][0], cot_own[0][1])
+    z_trail_two = z_pair(z + 7, z + 1, False)
     arrived(*kv_p)
     kv_over_p = kv_send(over_own + p, y_right, y_left)
     kv_far += kv_send(yr * 4 + xh * 2 + p, y_left)
@@ -264,22 +271,20 @@
         lax.fori_loop(0, 3, tile, 0)
 
     forward(y)
-    arrived(*z_two[0])
-    z_three = [z_pair((z + 6) % 8, (z + 2) % 8, 0)]
+    arrived(*z_lead_two)
+    z_lead_three = z_pair(z + 6, z + 2, True)
     arrived(*kv_over_c)
     kv_far += kv_send(yl * 4 + (1 - xh) * 2 + c, y_right)
-    arrived(*z_two[1])
-    z_three.append(z_pair((z + 6) % 8, (z + 2) % 8, 1))
     arrived(*w_far)
     w_xh.append(copy(wt.at[y2 * 2 + xh], wt.at[y2 * 2 + xh], xh_peer))
+    arrived(*z_trail_two)
+    z_trail_three = z_pair(z + 6, z + 2, False)
     arrived(*kv_over_p)
     kv_far += kv_send(yr * 4 + (1 - xh) * 2 + p, y_left)
     forward(yl)
-    arrived(*z_three[0])
-    z_four = [copy(cot.at[(z + 5) % 8, 0], cot.at[(z + 5) % 8, 0], z_right)]
+    arrived(*z_lead_three)
+    z_four = z_pair(z + 5, z + 3, True)
     forward(yr)
-    arrived(*z_three[1])
-    z_four.append(copy(cot.at[(z + 3) % 8, 1], cot.at[(z + 3) % 8, 1], z_left))
     arrived(*kv_far)
     forward(y2)
 
@@ -293,6 +298,7 @@
             att[c, h, pl.ds(qi * HALF, HALF), :] = wide[:, h * HALF:(h + 1) * HALF].T.astype(BF16)
     att_core = copy(att.at[c], att.at[c], core_peer)
     arrived(*w_xh)
+    arrived(*z_trail_three)
 
     def w_block(i):
         return wt[(i % 4) * 2 + i // 4]
@@ -330,11 +336,11 @@
         return sends
 
     long_0 = out_hop(0, True, None)
-    short_1 = out_hop(1, False, None)
     arrived(*z_four)
 
     width_step(7, 0)
     pga_core = copy(pga.at[p], pga_in, core_peer)
+    short_1 = out_hop(1, False, None)
 
     def gw_term(x, yy):
         i = x * 4 + yy
@@ -427,7 +433,17 @@
 
     arrived(d_right[0], d_left[0])
     d_send[3, 1] = (df[over] + d_rin[1].astype(F32) + d_lin[1].astype(F32)).astype(BF16)
-    d_over = copy(d_send.at[3, 1], d_x, xh_peer)
+    sem_d = take(2)
+    d_over = [
+        pltpu.make_async_remote_copy(
+            src_ref=d_send.at[3, 1, h], dst_ref=d_x.at[c], send_sem=ss.at[sem_d + i],
+            recv_sem=rs.at[sem_d + i], device_id=to, device_id_type=MESH,
+        )
+        for i, (h, to) in enumerate(((c, xh_peer), (p, xh_cross)))
+    ]
+    for d in d_over:
+        d.start()
+    sent.extend(d_over)
 
     first = c == 0
 
@@ -442,6 +458,14 @@
     arrived(*short_3)
     for h in range(2):
         out_fin[h] = out_term(z, h) + out_in[1 - h, 3, h].astype(F32)
+    gw_ref[...] = gw_term(xh, y) + gw_xin[3].astype(F32)
+
+    arrived(d_right[1], d_left[1])
+    for part in range(2):
+        total = df[near, part] + d_rin[0, :, part].astype(F32) + d_lin[0, :, part].astype(F32)
+        fin[:, part] = total
+    fin_core = copy(fin.at[p], fin_in, core_peer)
+
     arrived(*long_3)
     for h in range(2):
         out_send[0, 4, h] = (out_fin[h] + out_in[h, 3, h].astype(F32)).astype(BF16)
@@ -467,29 +491,16 @@
         to_peers[0].start()
         to_peers[1].start()
 
-    arrived(d_right[1], d_left[1])
-    arrived(d_over)
-    for part in range(2):
-        total = (
-            df[near, part]
-            + d_rin[0, :, part].astype(F32)
-            + d_lin[0, :, part].astype(F32)
-            + d_x[:, part].astype(F32)
-        )
-        fin[:, part] = total * SCALE if part == 0 else total
-    fin_core = copy(fin.at[p], fin_in, core_peer)
-
     arrived(*gw_near)
-    gw_ref[...] = (
-        gw_term(xh, y) + gw_xin[3].astype(F32) + gw_rin[...].astype(F32) + gw_lin[...].astype(F32)
-    )
+    gw_ref[...] += gw_rin[...].astype(F32) + gw_lin[...].astype(F32)
     store(4, gw_ref, gw_hbm)
 
-    arrived(fin_core)
-    place(dk_ref, fin[c, 0], fin_in[0])
-    store(2, dk_ref, dk_hbm)
-    place(dv_ref, fin[c, 1], fin_in[1])
-    store(3, dv_ref, dv_hbm)
+    arrived(fin_core, *d_over)
+    for i, (ref, factor) in enumerate(((dk_ref, SCALE), (dv_ref, 1.0))):
+        mine = (fin[c, i] + d_x[c, i].astype(F32)) * factor
+        theirs = (fin_in[i] + d_x[p, i].astype(F32)) * factor
+        place(ref, mine, theirs)
+        store(2 + i, ref, (dk_hbm, dv_hbm)[i])
 
     arrived(to_peers[0])
 
@@ -510,8 +521,8 @@
                 d.wait_send()
 
     cot_ici.wait_send()
-    for d in cot_z:
-        d.wait_send()
+    cot_lead.wait_send()
+    cot_trail.wait_send()
 
     store(0, out_ref, out_hbm)
     for d in sent:

time: 81.5 us -> 79.8 us (0.979)
  Pallas kernels: 80.7 us -> 79 us
    pallas_call x1, Pallas kernels: 78.6 us -> 76.8 us  [fused(): pl.pallas_call(kernel, name='attention_core', out_shape=OUT_SHAPES, in_sp...]
where the time goes in v4:
time: 79.8 us; the launch traced here: 79.6 us
  Pallas kernels  79 us (99%)
    pallas_call x1, Pallas kernels, fused(): pl.pallas_call(kernel, name='attention_core', out_shape=OUT_SHAPES, in_sp...  76.8 us
    pallas_call x1, Pallas kernels, stored(): pl.pallas_call(store_kernel, name='store_results', out_shape=OUT_SHAPES,...  2.15 us

profile of v4, /device:TPU:1, one launch (start us, length us, event | category | flops | bytes accessed | tf_op | source)
XLA Modules:
  0.0 79.6 jit_solution(7905663300865384962)
XLA Ops:
  0.6 76.8 %attention_core.1 = (f32[320,256]{1,0:T(8,128)}, f32[256,256]{1,0:T(8,128)}, f32[256,256]{1,0:T(8,128)}, f32[256,256]{1,0:T(8,128)}, f32[320,256]{1,0:T(8,128)}) custom-call(s32[256]{0:T(256)} %pos_ref.1, bf16[256,256]{1,0:T(8,128)(2,1)} %q_ref.1, bf16[256,256]{1,0:T(8,128)(2,1)} %k_ref.1, bf16[256,256]{1,0:T(8,128)(2,1)} %v_ref.1, ...), custom_call_target="tpu_custom_call" | custom-call | tf_op jit(solution)/shard_map/attention_core/pallas_call | solution.py:584
  77.5 2.2 %store_results.1 = (f32[320,256]{1,0:T(8,128)}, f32[256,256]{1,0:T(8,128)}, f32[256,256]{1,0:T(8,128)}, f32[256,256]{1,0:T(8,128)}, f32[320,256]{1,0:T(8,128)}) custom-call(f32[320,256]{1,0:T(8,128)} %get-tuple-element.15.refs_0_, f32[256,256]{1,0:T(8,128)} %get-tuple-element.16.refs_1_, f32[256,256]{1,0:T(8,128)} %get-tuple-element.17.refs_2_, ...), custom_call_target="tpu_custom_call" | custom-call | tf_op jit(solution)/shard_map/store_results/pallas_call | solution.py:620

commit v5 on v4

--- a/solution.py
+++ b/solution.py
@@ -322,10 +322,11 @@
 
     def out_hop(step, long_chain, got):
         sends = []
-        for side in range(2):
-            h = side if long_chain else 1 - side
-            target = (z + 4 - step) % 8 if side == 0 else (z + 4 + step) % 8
-            term = out_term(target, h)
+        halves = (0, 1) if long_chain else (1, 0)
+        targets = ((z + 4 - step) % 8, (z + 4 + step) % 8)
+        terms = [out_term(targets[side], halves[side]) for side in range(2)]
+        for side, h in enumerate(halves):
+            term = terms[side]
             if got is not None:
                 arrived(got[side])
                 term = term + out_in[side, step - 1, h].astype(F32)
@@ -340,7 +341,6 @@
 
     width_step(7, 0)
     pga_core = copy(pga.at[p], pga_in, core_peer)
-    short_1 = out_hop(1, False, None)
 
     def gw_term(x, yy):
         i = x * 4 + yy
@@ -351,6 +351,7 @@
         gw_xsend[i] = gw_term(1 - xh, yy).astype(BF16)
         gw_over.append(copy(gw_xsend.at[i], gw_xin.at[i], xh_peer))
 
+    short_1 = out_hop(1, False, None)
     arrived(pga_core)
     for h in range(2):
         rows = (pga[c, h] + pga_in[h]).astype(BF16)
@@ -400,8 +401,8 @@
     backward(yr, df_right)
     d_send[1, 1] = df_right[over].astype(BF16)
     d_right = [copy(d_send.at[1, 1], d_rin.at[1], y_right)]
+    backward(yl, df)
     short_2 = out_hop(2, False, short_1)
-    backward(yl, df)
     arrived(d_far_left)
     d_send[2, 1] = (df[over] + d_lin2[...].astype(F32)).astype(BF16)
     d_left = [copy(d_send.at[2, 1], d_lin.at[1], y_left)]

time: 79.8 us -> 79.3 us (level)
  no operation moved by 1% of the time
where the time goes in v5:
time: 79.3 us; the launch traced here: 79.2 us
  Pallas kernels  78.5 us (99%)
    pallas_call x1, Pallas kernels, fused(): pl.pallas_call(kernel, name='attention_core', out_shape=OUT_SHAPES, in_sp...  76.4 us
    pallas_call x1, Pallas kernels, stored(): pl.pallas_call(store_kernel, name='store_results', out_shape=OUT_SHAPES,...  2.15 us

profile of v5, /device:TPU:1, one launch (start us, length us, event | category | flops | bytes accessed | tf_op | source)
XLA Modules:
  0.0 79.2 jit_solution(14720060316796619294)
XLA Ops:
  0.6 76.4 %attention_core.1 = (f32[320,256]{1,0:T(8,128)}, f32[256,256]{1,0:T(8,128)}, f32[256,256]{1,0:T(8,128)}, f32[256,256]{1,0:T(8,128)}, f32[320,256]{1,0:T(8,128)}) custom-call(s32[256]{0:T(256)} %pos_ref.1, bf16[256,256]{1,0:T(8,128)(2,1)} %q_ref.1, bf16[256,256]{1,0:T(8,128)(2,1)} %k_ref.1, bf16[256,256]{1,0:T(8,128)(2,1)} %v_ref.1, ...), custom_call_target="tpu_custom_call" | custom-call | tf_op jit(solution)/shard_map/attention_core/pallas_call | solution.py:585
  77.0 2.2 %store_results.1 = (f32[320,256]{1,0:T(8,128)}, f32[256,256]{1,0:T(8,128)}, f32[256,256]{1,0:T(8,128)}, f32[256,256]{1,0:T(8,128)}, f32[320,256]{1,0:T(8,128)}) custom-call(f32[320,256]{1,0:T(8,128)} %get-tuple-element.15.refs_0_, f32[256,256]{1,0:T(8,128)} %get-tuple-element.16.refs_1_, f32[256,256]{1,0:T(8,128)} %get-tuple-element.17.refs_2_, ...), custom_call_target="tpu_custom_call" | custom-call | tf_op jit(solution)/shard_map/store_results/pallas_call | solution.py:621

commit v6 on v5

--- a/solution.py
+++ b/solution.py
@@ -401,8 +401,8 @@
     backward(yr, df_right)
     d_send[1, 1] = df_right[over].astype(BF16)
     d_right = [copy(d_send.at[1, 1], d_rin.at[1], y_right)]
+    short_2 = out_hop(2, False, short_1)
     backward(yl, df)
-    short_2 = out_hop(2, False, short_1)
     arrived(d_far_left)
     d_send[2, 1] = (df[over] + d_lin2[...].astype(F32)).astype(BF16)
     d_left = [copy(d_send.at[2, 1], d_lin.at[1], y_left)]

time: 79.3 us -> 79.3 us (level)
  no operation moved by 1% of the time
where the time goes in v6:
time: 79.3 us; the launch traced here: 79.2 us
  Pallas kernels  78.5 us (99%)
    pallas_call x1, Pallas kernels, fused(): pl.pallas_call(kernel, name='attention_core', out_shape=OUT_SHAPES, in_sp...  76.4 us
    pallas_call x1, Pallas kernels, stored(): pl.pallas_call(store_kernel, name='store_results', out_shape=OUT_SHAPES,...  2.15 us

profile of v6, /device:TPU:1, one launch (start us, length us, event | category | flops | bytes accessed | tf_op | source)
XLA Modules:
  0.0 79.2 jit_solution(6027056190607127867)
XLA Ops:
  0.6 76.4 %attention_core.1 = (f32[320,256]{1,0:T(8,128)}, f32[256,256]{1,0:T(8,128)}, f32[256,256]{1,0:T(8,128)}, f32[256,256]{1,0:T(8,128)}, f32[320,256]{1,0:T(8,128)}) custom-call(s32[256]{0:T(256)} %pos_ref.1, bf16[256,256]{1,0:T(8,128)(2,1)} %q_ref.1, bf16[256,256]{1,0:T(8,128)(2,1)} %k_ref.1, bf16[256,256]{1,0:T(8,128)(2,1)} %v_ref.1, ...), custom_call_target="tpu_custom_call" | custom-call | tf_op jit(solution)/shard_map/attention_core/pallas_call | solution.py:585
  77.0 2.2 %store_results.1 = (f32[320,256]{1,0:T(8,128)}, f32[256,256]{1,0:T(8,128)}, f32[256,256]{1,0:T(8,128)}, f32[256,256]{1,0:T(8,128)}, f32[320,256]{1,0:T(8,128)}) custom-call(f32[320,256]{1,0:T(8,128)} %get-tuple-element.15.refs_0_, f32[256,256]{1,0:T(8,128)} %get-tuple-element.16.refs_1_, f32[256,256]{1,0:T(8,128)} %get-tuple-element.17.refs_2_, ...), custom_call_target="tpu_custom_call" | custom-call | tf_op jit(solution)/shard_map/store_results/pallas_call | solution.py:621
